TPU v7x, 32 devices: a whole 2x2x4 slice. The times are simulated.
32 devices in a mesh: field: 2 (over y), expo: 8 (over z, core), strip: 2 (over x).
Axes of the slice: x: 2, y: 2, z: 4, core: 2. Of those that a mesh axis runs over, the one named last changes fastest.
Arguments:
- science: bfloat16 [128, 64, 512], P(('field', 'expo'), 'strip'), parts along dimension 0, may hold values from -6 to 6
- inv_var: bfloat16 [128, 64, 512], P(('field', 'expo'), 'strip'), parts along dimension 0, may hold values from 0.25 to 4
- psf_rows: float32 [128, 9], P(('field', 'expo')), parts along dimension 0, may hold values from 0.2 to 1
- psf_cols: float32 [128, 9], P(('field', 'expo')), parts along dimension 0, may hold values from 0.2 to 1
- row_shift: int32 [128, 8], P(('field', 'expo')), parts along dimension 0, may hold values from 0 to 16
- col_shift: int32 [128, 8], P(('field', 'expo')), parts along dimension 0, may hold values from -16 to 16
- exposure_ok: int32 [128], P(('field', 'expo')), parts along dimension 0, may hold values 0 or 1
Outputs:
- likelihood: float32 [2, 16, 32, 512], P('strip', 'field', 'expo'), parts along dimension 1
There are 2 independent parts, one for each index of `field`. A program takes and returns all parts, laid end to end along the dimension named above; each array names one. Nothing has to cross between parts.
Inputs may be any that keep to these rules, and one draw needn't show every extreme that they name: `row_shift`: every shift lies in 0..16, so S[e, v, r] reads map rows r to r + 16 only, never lower rows.
All inputs are finite; a program needn't handle non-finite values. No bound on the sum of `exposure_ok` on one device may be relied on, other than what follows from the above.
Results may differ from a plain program's by a relative error of at most 0.0017.
Values may be sent and summed in bfloat16 or wider, within the bound.
A program may use at most 64 MiB of HBM per device.

v0:
```python
import jax
import jax.numpy as jnp
from jax import lax
from jax.sharding import PartitionSpec as P

SHIFT = 16


def extended_2(cells, sides, width):
    for axis, dim in sides:
        count = lax.axis_size(axis)
        ends = count - 1
        head = lax.slice_in_dim(cells, 0, width, axis=dim)
        tail = lax.slice_in_dim(cells, cells.shape[dim] - width, cells.shape[dim], axis=dim)
        cells = jnp.concatenate(
            [
                lax.ppermute(tail, axis, [(i, (i + 1) % count) for i in range(ends)]),
                cells,
                lax.ppermute(head, axis, [((i + 1) % count, i) for i in range(ends)]),
            ],
            axis=dim,
        )
    return cells


def filter_one(picture, row_taps, col_taps, out_rows):
    columns = picture.shape[2]
    tap_count = row_taps.shape[1]
    radius = tap_count // 2
    padded = jnp.pad(picture, ((0, 0), (0, 0), (radius, radius)))
    colpass = col_taps[:, 0, None, None] * padded[:, :, 0:columns]
    for b in range(1, tap_count):
        colpass = colpass + col_taps[:, b, None, None] * padded[:, :, b : b + columns]
    result = row_taps[:, 0, None, None] * colpass[:, 0:out_rows]
    for a in range(1, tap_count):
        result = result + row_taps[:, a, None, None] * colpass[:, a : a + out_rows]
    return result.astype(jnp.bfloat16)


def matched_pair(science, inv_var, psf_rows, psf_cols, out_rows):
    science_f = science.astype(jnp.float32)
    inverse = inv_var.astype(jnp.float32)
    signal_map = filter_one(science_f * inverse, psf_rows, psf_cols, out_rows)
    depth_map = filter_one(inverse, psf_rows * psf_rows, psf_cols * psf_cols, out_rows)
    return (signal_map, depth_map)


def per_device(science, inv_var, psf_rows, psf_cols, row_shift, col_shift, exposure_ok):
    local_rows = science.shape[1]
    columns = science.shape[2]
    vel_count = row_shift.shape[1]
    radius = psf_rows.shape[1] // 2
    stacked = jnp.stack([science, inv_var])
    extended = extended_2(stacked, (("strip", 2),), radius + SHIFT)
    inner_rows = extended[:, :, SHIFT:]
    signal_map, depth_map = matched_pair(
        inner_rows[0], inner_rows[1], psf_rows, psf_cols, local_rows + SHIFT
    )
    row_keep = (lax.iota(jnp.int32, local_rows + SHIFT) < local_rows) | (
        lax.axis_index("strip") < lax.axis_size("strip") - 1
    )
    row_keep = row_keep[None, :, None]
    signal_map = jnp.where(row_keep, signal_map, jnp.zeros_like(signal_map))
    depth_map = jnp.where(row_keep, depth_map, jnp.zeros_like(depth_map))
    pair_maps = jnp.stack([signal_map, depth_map], 1)
    padded = jnp.pad(pair_maps, ((0, 0), (0, 0), (0, 0), (SHIFT, SHIFT)))
    usable = exposure_ok.astype(jnp.float32)[:, None, None, None]

    def cut_one(maps_block, row_at, col_at):
        return lax.dynamic_slice(
            maps_block, (jnp.zeros((), jnp.int32), row_at, col_at + SHIFT), (2, local_rows, columns)
        )

    def cut_all(velocity):
        return jax.vmap(cut_one)(padded, row_shift[:, velocity], col_shift[:, velocity]).astype(
            jnp.float32
        )

    first_sums = jnp.stack(
        [jnp.sum(usable * cut_all(velocity), axis=0) for velocity in range(vel_count)]
    )
    whole_sums = lax.psum((first_sums[:, 0], first_sums[:, 1]), "expo")
    flux_est = whole_sums[0] / (whole_sums[1] + 1.0)
    robust_signal = []
    robust_depth = []
    for velocity in range(vel_count):
        windows_now = cut_all(velocity)
        signal = windows_now[:, 0]
        depth = windows_now[:, 1]
        residual = signal - flux_est[velocity][None] * depth
        weight = usable[:, 0] / (1.0 + residual * residual / (depth + 1.0))
        robust_signal.append(jnp.sum(weight * signal, axis=0))
        robust_depth.append(jnp.sum(weight * depth, axis=0))
    robust = (
        lax.psum_scatter(jnp.stack(robust_signal), "expo", scatter_dimension=1, tiled=True),
        lax.psum_scatter(jnp.stack(robust_depth), "expo", scatter_dimension=1, tiled=True),
    )
    likelihood = robust[0] / jnp.sqrt(robust[1] + 1.0)
    return likelihood[None]


def solution(mesh):
    in_specs = (
        P(("field", "expo"), "strip", None),
        P(("field", "expo"), "strip", None),
        P(("field", "expo"), None),
        P(("field", "expo"), None),
        P(("field", "expo"), None),
        P(("field", "expo"), None),
        P(("field", "expo")),
    )
    out_specs = P("strip", "field", "expo", None)
    return jax.shard_map(
        per_device, mesh=mesh, in_specs=in_specs, out_specs=out_specs, check_vma=False
    )
```

profile of v0, /device:TPU:0, one launch (start us, length us, event | category | flops | bytes accessed | tf_op | source)
XLA Modules:
  0.0 360.9 jit_solution(3347741036529363502)
XLA Ops:
  8.1 4.9 %collective-permute-start = (bf16[2,8,20,512]{3,2,1,0:T(8,128)(2,1)S(1)}, bf16[2,8,20,512]{3,2,1,0:T(8,128)(2,1)S(1)}, u32[]{:S(2)}, u32[]{:S(2)}) collective-permute-start(bf16[2,8,20,512]{3,2,1,0:T(8,128)(2,1)S(1)} %get-tuple-element.229), channel_id=1, source_target_pairs={{0,1},{2,3},{4,5},{6,7},{8,9},{10,11},{12,13},{14,15},{16,17},{18,... | collective-permute-start | bytes 983048 | tf_op jit(solution)/shard_map/ppermute | solution.py:17
  17.1 4.1 %collective-permute-done = bf16[2,8,20,512]{3,2,1,0:T(8,128)(2,1)S(1)} collective-permute-done((bf16[2,8,20,512]{3,2,1,0:T(8,128)(2,1)S(1)}, bf16[2,8,20,512]{3,2,1,0:T(8,128)(2,1)S(1)}, u32[]{:S(2)}, u32[]{:S(2)}) %collective-permute-start) | collective-permute-done | bytes 327712 | tf_op jit(solution)/shard_map/ppermute | solution.py:17
  21.3 4.1 %collective-permute-done.1 = bf16[2,8,20,512]{3,2,1,0:T(8,128)(2,1)S(1)} collective-permute-done((bf16[2,8,20,512]{3,2,1,0:T(8,128)(2,1)S(1)}, bf16[2,8,20,512]{3,2,1,0:T(8,128)(2,1)S(1)}, u32[]{:S(2)}, u32[]{:S(2)}) %collective-permute-start.1) | collective-permute-done | bytes 327712 | tf_op jit(solution)/shard_map/ppermute | solution.py:19
  25.7 2.1 fusion.12
  27.9 2.1 fusion.28
  32.5 21.5 %while.8 = (s32[]{:T(128)}, bf16[8,2,48,544]{3,2,1,0:T(8,128)(2,1)S(1)}, s32[8,4]{0,1:T(4,128)S(1)}, bf16[8,2,32,512]{3,2,0,1:T(8,128)(2,1)S(1)}, s32[]{:T(128)}) while((s32[]{:T(128)}, bf16[8,2,48,544]{3,2,1,0:T(8,128)(2,1)S(1)}, s32[8,4]{0,1:T(4,128)S(1)}, bf16[8,2,32,512]{3,2,0,1:T(8,128)(2,1)S(1)}, s32[]{:T(128)}) %tuple.233), condition=%wide.while_cond, body=%wide.while_body.sunk | while | flops 2 | bytes 131209 | solution.py:70
  33.2 2.0 bitcast_dynamic-update-slice_fusion.22
  35.9 2.0 bitcast_dynamic-update-slice_fusion.22
  41.3 2.0 bitcast_dynamic-update-slice_fusion.22
  44.0 2.0 bitcast_dynamic-update-slice_fusion.22
  46.7 2.0 bitcast_dynamic-update-slice_fusion.22
  49.4 2.0 bitcast_dynamic-update-slice_fusion.22
  54.1 21.0 %while.9 = (s32[]{:T(128)}, bf16[8,2,48,544]{3,2,1,0:T(8,128)(2,1)S(1)}, s32[8,4]{0,1:T(4,128)S(1)}, bf16[8,2,32,512]{3,2,0,1:T(8,128)(2,1)S(1)}, s32[]{:T(128)}) while((s32[]{:T(128)}, bf16[8,2,48,544]{3,2,1,0:T(8,128)(2,1)S(1)}, s32[8,4]{0,1:T(4,128)S(1)}, bf16[8,2,32,512]{3,2,0,1:T(8,128)(2,1)S(1)}, s32[]{:T(128)}) %tuple.246), condition=%wide.while_cond.1, body=%wide.while_body.1.sunk | while | flops 2 | bytes 131209 | solution.py:70
  75.2 20.7 %while.10 = (s32[]{:T(128)}, bf16[8,2,48,544]{3,2,1,0:T(8,128)(2,1)S(1)}, s32[8,4]{0,1:T(4,128)S(1)}, bf16[8,2,32,512]{3,2,0,1:T(8,128)(2,1)S(1)}, s32[]{:T(128)}) while((s32[]{:T(128)}, bf16[8,2,48,544]{3,2,1,0:T(8,128)(2,1)S(1)}, s32[8,4]{0,1:T(4,128)S(1)}, bf16[8,2,32,512]{3,2,0,1:T(8,128)(2,1)S(1)}, s32[]{:T(128)}) %tuple.247), condition=%wide.while_cond.2, body=%wide.while_body.2.sunk | while | flops 2 | bytes 131209 | solution.py:70
  96.8 25.5 %while.11 = (s32[]{:T(128)}, bf16[8,2,48,544]{3,2,1,0:T(8,128)(2,1)S(1)}, s32[8,4]{0,1:T(4,128)S(1)}, bf16[8,2,32,512]{3,2,0,1:T(8,128)(2,1)}, s32[]{:T(128)}) while((s32[]{:T(128)}, bf16[8,2,48,544]{3,2,1,0:T(8,128)(2,1)S(1)}, s32[8,4]{0,1:T(4,128)S(1)}, bf16[8,2,32,512]{3,2,0,1:T(8,128)(2,1)}, s32[]{:T(128)}) %tuple.248), condition=%wide.while_cond.3, body=%wide.while_body.3.sunk | while | flops 2 | bytes 133241 | solution.py:70
  97.5 2.5 bitcast_dynamic-update-slice_fusion.25
  100.7 2.5 bitcast_dynamic-update-slice_fusion.25
  103.9 2.5 bitcast_dynamic-update-slice_fusion.25
  107.1 2.5 bitcast_dynamic-update-slice_fusion.25
  110.3 2.5 bitcast_dynamic-update-slice_fusion.25
  113.4 2.5 bitcast_dynamic-update-slice_fusion.25
  116.6 2.5 bitcast_dynamic-update-slice_fusion.25
  119.8 2.5 bitcast_dynamic-update-slice_fusion.25
  123.2 26.1 %while.12 = (s32[]{:T(128)}, bf16[8,2,48,544]{3,2,1,0:T(8,128)(2,1)S(1)}, s32[8,4]{0,1:T(4,128)S(1)}, bf16[8,2,32,512]{3,2,0,1:T(8,128)(2,1)}, s32[]{:T(128)}) while((s32[]{:T(128)}, bf16[8,2,48,544]{3,2,1,0:T(8,128)(2,1)S(1)}, s32[8,4]{0,1:T(4,128)S(1)}, bf16[8,2,32,512]{3,2,0,1:T(8,128)(2,1)}, s32[]{:T(128)}) %tuple.249), condition=%wide.while_cond.4, body=%wide.while_body.4.sunk | while | flops 2 | bytes 133241 | solution.py:70
  123.9 2.6 bitcast_dynamic-update-slice_fusion.26
  127.1 2.6 bitcast_dynamic-update-slice_fusion.26
  130.4 2.6 bitcast_dynamic-update-slice_fusion.26
  133.7 2.6 bitcast_dynamic-update-slice_fusion.26
  136.9 2.6 bitcast_dynamic-update-slice_fusion.26
  140.2 2.6 bitcast_dynamic-update-slice_fusion.26
  143.5 2.6 bitcast_dynamic-update-slice_fusion.26
  146.7 2.6 bitcast_dynamic-update-slice_fusion.26
  150.2 25.7 %while.13 = (s32[]{:T(128)}, bf16[8,2,48,544]{3,2,1,0:T(8,128)(2,1)S(1)}, s32[8,4]{0,1:T(4,128)S(1)}, bf16[8,2,32,512]{3,2,0,1:T(8,128)(2,1)}, s32[]{:T(128)}) while((s32[]{:T(128)}, bf16[8,2,48,544]{3,2,1,0:T(8,128)(2,1)S(1)}, s32[8,4]{0,1:T(4,128)S(1)}, bf16[8,2,32,512]{3,2,0,1:T(8,128)(2,1)}, s32[]{:T(128)}) %tuple.250), condition=%wide.while_cond.5, body=%wide.while_body.5.sunk | while | flops 2 | bytes 133241 | solution.py:70
  150.9 2.5 bitcast_dynamic-update-slice_fusion.27
  154.1 2.5 bitcast_dynamic-update-slice_fusion.27
  157.3 2.5 bitcast_dynamic-update-slice_fusion.27
  160.5 2.6 bitcast_dynamic-update-slice_fusion.27
  163.7 2.6 bitcast_dynamic-update-slice_fusion.27
  166.9 2.6 bitcast_dynamic-update-slice_fusion.27
  170.1 2.6 bitcast_dynamic-update-slice_fusion.27
  173.3 2.6 bitcast_dynamic-update-slice_fusion.27
  175.9 20.8 %while.15 = (s32[]{:T(128)}, bf16[8,2,48,544]{3,2,1,0:T(8,128)(2,1)S(1)}, s32[8,4]{0,1:T(4,128)S(1)}, bf16[8,2,32,512]{3,2,1,0:T(8,128)(2,1)S(1)}, s32[]{:T(128)}) while((s32[]{:T(128)}, bf16[8,2,48,544]{3,2,1,0:T(8,128)(2,1)S(1)}, s32[8,4]{0,1:T(4,128)S(1)}, bf16[8,2,32,512]{3,2,1,0:T(8,128)(2,1)S(1)}, s32[]{:T(128)}) %tuple.251), condition=%wide.while_cond.7, body=%wide.while_body.7.sunk | while | flops 2 | bytes 131209 | solution.py:70
  196.8 21.5 %while.14 = (s32[]{:T(128)}, bf16[8,2,48,544]{3,2,1,0:T(8,128)(2,1)S(1)}, s32[8,4]{0,1:T(4,128)S(1)}, bf16[8,2,32,512]{3,2,0,1:T(8,128)(2,1)S(1)}, s32[]{:T(128)}) while((s32[]{:T(128)}, bf16[8,2,48,544]{3,2,1,0:T(8,128)(2,1)S(1)}, s32[8,4]{0,1:T(4,128)S(1)}, bf16[8,2,32,512]{3,2,0,1:T(8,128)(2,1)S(1)}, s32[]{:T(128)}) %tuple.252), condition=%wide.while_cond.6, body=%wide.while_body.6.sunk | while | flops 2 | bytes 131209 | solution.py:70
  218.3 2.7 multiply_reduce_fusion
  231.3 50.5 %all-reduce.6.cloned.1.call-done = (f32[8,32,512]{2,1,0:T(8,128)}, f32[8,32,512]{2,1,0:T(8,128)}) async-done(((f32[8,32,512]{2,1,0:T(8,128)}, f32[8,32,512]{2,1,0:T(8,128)}), (f32[8,32,512]{2,1,0:T(8,128)}, f32[8,32,512]{2,1,0:T(8,128)})) %all-reduce.6.cloned.1.call-update) | async-done | bytes 1048592 | tf_op jit(solution)/shard_map/psum | solution.py:82
  283.7 2.1 add_divide_fusion
  293.2 28.0 %reduce-scatter.5.cloned.1.call-done = f32[8,4,512]{2,0,1:T(8,128)} async-done(((f32[8,32,512]{2,0,1:T(8,128)}), f32[8,4,512]{2,0,1:T(8,128)}) %reduce-scatter.5.cloned.1.call-update) | async-done | bytes 65552 | tf_op jit(solution)/shard_map/reduce_scatter | solution.py:96
  321.2 31.5 %reduce-scatter.3.cloned.1.call-done = f32[8,4,512]{2,0,1:T(8,128)} async-done(((f32[8,32,512]{2,0,1:T(8,128)}), f32[8,4,512]{2,0,1:T(8,128)}) %reduce-scatter.3.cloned.1.call-update) | async-done | bytes 65552 | tf_op jit(solution)/shard_map/reduce_scatter | solution.py:95
  (319 shorter events, 140.6 us)
Async XLA Ops:
  6.5 18.9 %copy-start.17 = (bf16[8,32,512]{2,1,0:T(8,128)(2,1)S(1)}, bf16[8,32,512]{2,1,0:T(8,128)(2,1)}, u32[]{:S(2)}) copy-start(bf16[8,32,512]{2,1,0:T(8,128)(2,1)} %param.7) | copy-start | bytes 786436
  6.5 18.9 %copy-start.18 = (bf16[8,32,512]{2,1,0:T(8,128)(2,1)S(1)}, bf16[8,32,512]{2,1,0:T(8,128)(2,1)}, u32[]{:S(2)}) copy-start(bf16[8,32,512]{2,1,0:T(8,128)(2,1)} %param.8) | copy-start | bytes 786436
  6.5 7.7 %copy-start.19 = (f32[8,9]{1,0:T(8,128)S(1)}, f32[8,9]{1,0:T(8,128)}, u32[]{:S(2)}) copy-start(f32[8,9]{1,0:T(8,128)} %param.10) | copy-start | bytes 868
  6.5 8.0 %copy-start.20 = (f32[8,9]{1,0:T(8,128)S(1)}, f32[8,9]{1,0:T(8,128)}, u32[]{:S(2)}) copy-start(f32[8,9]{1,0:T(8,128)} %param.9) | copy-start | bytes 868
  6.5 8.3 %copy-start.21 = (s32[8,8]{1,0:T(8,128)S(1)}, s32[8,8]{1,0:T(8,128)}, u32[]{:S(2)}) copy-start(s32[8,8]{1,0:T(8,128)} %param.11) | copy-start | bytes 772
  6.5 8.5 %copy-start.22 = (s32[8,8]{1,0:T(8,128)S(1)}, s32[8,8]{1,0:T(8,128)}, u32[]{:S(2)}) copy-start(s32[8,8]{1,0:T(8,128)} %param.12) | copy-start | bytes 772
  6.6 9.8 %copy-start.24 = (s32[8]{0:T(128)S(1)}, s32[8]{0:T(128)}, u32[]{:S(2)}) copy-start(s32[8]{0:T(128)} %param.13) | copy-start | bytes 100
  6.6 275.2 %all-reduce.6.cloned.1.call-start = ((), (), s32[]{:S(2)}) async-start(), calls=%async_computation.4 | async-start | bytes 2097152 | tf_op jit(solution)/shard_map/psum | solution.py:82
  8.1 13.2 %collective-permute-start = (bf16[2,8,20,512]{3,2,1,0:T(8,128)(2,1)S(1)}, bf16[2,8,20,512]{3,2,1,0:T(8,128)(2,1)S(1)}, u32[]{:S(2)}, u32[]{:S(2)}) collective-permute-start(bf16[2,8,20,512]{3,2,1,0:T(8,128)(2,1)S(1)} %get-tuple-element.229), channel_id=1, source_target_pairs={{0,1},{2,3},{4,5},{6,7},{8,9},{10,11},{12,13},{14,15},{16,17},{18,... | collective-permute-start | bytes 983048 | tf_op jit(solution)/shard_map/ppermute | solution.py:17
  12.9 12.5 %collective-permute-start.1 = (bf16[2,8,20,512]{3,2,1,0:T(8,128)(2,1)S(1)}, bf16[2,8,20,512]{3,2,1,0:T(8,128)(2,1)S(1)}, u32[]{:S(2)}, u32[]{:S(2)}) collective-permute-start(bf16[2,8,20,512]{3,2,1,0:T(8,128)(2,1)S(1)} %get-tuple-element.230), channel_id=1, source_target_pairs={{1,0},{3,2},{5,4},{7,6},{9,8},{11,10},{13,12},{15,14},{17,16},{19,... | collective-permute-start | bytes 983048 | tf_op jit(solution)/shard_map/ppermute | solution.py:19
  54.1 164.2 %copy-start.9 = (bf16[8,2,32,512]{3,2,0,1:T(8,128)(2,1)}, bf16[8,2,32,512]{3,2,0,1:T(8,128)(2,1)S(1)}, u32[]{:S(2)}) copy-start(bf16[8,2,32,512]{3,2,0,1:T(8,128)(2,1)S(1)} %get-tuple-element.12) | copy-start | bytes 1572868
  95.9 100.8 %copy-start.11 = (bf16[8,2,32,512]{3,2,0,1:T(8,128)(2,1)}, bf16[8,2,32,512]{3,2,0,1:T(8,128)(2,1)S(1)}, u32[]{:S(2)}) copy-start(bf16[8,2,32,512]{3,2,0,1:T(8,128)(2,1)S(1)} %get-tuple-element.28) | copy-start | bytes 1572868
  196.7 24.3 %copy-start.4 = (bf16[8,2,32,512]{3,2,1,0:T(8,128)(2,1)}, bf16[8,2,32,512]{3,2,1,0:T(8,128)(2,1)S(1)}, u32[]{:S(2)}) copy-start(bf16[8,2,32,512]{3,2,1,0:T(8,128)(2,1)S(1)} %get-tuple-element.68) | copy-start | bytes 1572868
  218.3 2.8 copy-start.7
  222.3 98.9 %reduce-scatter.5.cloned.1.call-start = ((), (), s32[]{:S(2)}) async-start(), calls=%async_computation.3 | async-start | bytes 589824 | tf_op jit(solution)/shard_map/reduce_scatter | solution.py:96
  222.5 1.0 copy-start.12
  223.5 1.0 copy-start.13
  224.6 1.0 copy-start.14
  225.6 1.2 copy-start.15
  226.8 1.1 copy-start.5
  227.9 1.1 copy-start.10
  229.0 1.1 copy-start.8
  281.7 1.5 copy-start
  281.7 1.9 copy-start.1
  281.7 2.0 copy-start.6
  283.7 2.1 copy-start.16
  287.3 1.2 copy-start.3
  287.5 1.4 copy-start.2
  289.6 1.8 copy-start.23
  291.2 61.6 %reduce-scatter.3.cloned.1.call-start = ((), (), s32[]{:S(2)}) async-start(), calls=%async_computation.2 | async-start | bytes 589824 | tf_op jit(solution)/shard_map/reduce_scatter | solution.py:95
Sparse Core Ops, SparseCore 0:
  222.4 59.2 all-reduce.5
  291.3 29.8 reduce-scatter.4
  323.6 29.1 reduce-scatter.2
where the time goes:
time: 363 us; the launch traced here: 361 us
  local copies, waits for them, and re-layouts  198 us (55%)
  waiting for transfers between devices  118 us (33%)
  other arithmetic  23.9 us (7%)
  between operations  13.9 us (4%)
  starting transfers between devices  6.46 us (2%)
    gather x192, local copies, waits for them, and re-layouts  182 us
    psum x1, waiting for transfers between devices, per_device(): whole_sums = lax.psum((first_sums[:, 0], first_sums[:, 1]), 'expo')  50.5 us
    reduce_scatter x1, waiting for transfers between devices, per_device(): lax.psum_scatter(jnp.stack(robust_signal), 'expo', scatter_dimension=1, t...  31.5 us
    reduce_scatter x1, waiting for transfers between devices, per_device(): lax.psum_scatter(jnp.stack(robust_depth), 'expo', scatter_dimension=1, ti...  28 us
    unnamed x81, local copies, waits for them, and re-layouts  8.68 us
  transfers between devices with their start and end apart: 5, of which 5 were waited for; matrix products, arithmetic and copies ran while one was open for 3% of the time, Pallas kernels for 0%

commit v1 on v0

v1 whole, which is shorter than its diff:
```python
import functools

import jax
import jax.numpy as jnp
from jax import lax
from jax.experimental import pallas as pl
from jax.experimental.pallas import tpu as pltpu

SHIFT = 16
LANES = 128
MESH = pl.DeviceIdType.MESH


def roll4(x):
    return pltpu.roll(x, 4, axis=x.ndim - 2)


def kernel(
    cfg,
    row_taps, col_taps, row_shift, col_shift, usable, sci, inv,
    out,
    above, below, rows_in, maps, fluxes, *rest,
):
    count, strips, exposures, rows, columns, vels, taps = cfg
    radius = taps // 2
    chips = count // 2
    own = rows // count
    half = rows // 2
    blocks = columns // LANES
    groups = vels // 2
    wide = columns + LANES
    map_rows = rows + SHIFT
    sums, near, pair, far = zip(rest[0:4], rest[4:8])
    (halo_s, halo_r, near_s, near_r, far_s, far_r, flux_s, flux_r, fsib_s, fsib_r) = rest[8:]

    me = lax.axis_index("expo")
    strip = lax.axis_index("strip")
    chip, core = me // 2, me % 2
    sibling = chip * 2 + (1 - core)
    has_above = strip > 0
    has_below = strip < strips - 1

    def peer(j):
        return (chip + j) % chips

    def halo_copy(e, array, down):
        source = (sci, inv)[array]
        if down:
            src, dst, to = source.at[e, pl.ds(rows - 16, 16)], above.at[array, e], strip + 1
        else:
            src, dst, to = source.at[e], below.at[array, e], strip - 1
        slot = (1 if down else 0, array, e)
        return pltpu.make_async_remote_copy(
            src_ref=src, dst_ref=dst, send_sem=halo_s.at[slot], recv_sem=halo_r.at[slot],
            device_id={"strip": to}, device_id_type=MESH,
        )

    def near_copy(stage, g):
        return pltpu.make_async_remote_copy(
            src_ref=sums[stage].at[g, 1 - core], dst_ref=near[stage].at[g],
            send_sem=near_s.at[stage, g], recv_sem=near_r.at[stage, g],
            device_id={"expo": sibling}, device_id_type=MESH,
        )

    def far_copy(stage, g, j):
        return pltpu.make_async_remote_copy(
            src_ref=pair[stage].at[g, peer(j)], dst_ref=far[stage].at[g, j - 1],
            send_sem=far_s.at[stage, g, j - 1], recv_sem=far_r.at[stage, g, j - 1],
            device_id={"expo": peer(j) * 2 + core}, device_id_type=MESH,
        )

    def flux_copy(g, j):
        mine = fluxes.at[g, core, chip]
        return pltpu.make_async_remote_copy(
            src_ref=mine, dst_ref=mine,
            send_sem=flux_s.at[g, j - 1], recv_sem=flux_r.at[g, j - 1],
            device_id={"expo": peer(j) * 2 + core}, device_id_type=MESH,
        )

    def flux_sibling(g):
        mine = fluxes.at[g, core]
        return pltpu.make_async_remote_copy(
            src_ref=mine, dst_ref=mine, send_sem=fsib_s.at[g], recv_sem=fsib_r.at[g],
            device_id={"expo": sibling}, device_id_type=MESH,
        )

    barrier = pltpu.get_barrier_semaphore()
    pl.semaphore_signal(barrier, inc=1, device_id={"expo": sibling}, device_id_type=MESH)
    for j in range(1, chips):
        pl.semaphore_signal(
            barrier, inc=1, device_id={"expo": peer(j) * 2 + core}, device_id_type=MESH
        )

    @pl.when(has_above)
    def _():
        pl.semaphore_signal(barrier, inc=1, device_id={"strip": strip - 1}, device_id_type=MESH)

    @pl.when(has_below)
    def _():
        pl.semaphore_signal(barrier, inc=1, device_id={"strip": strip + 1}, device_id_type=MESH)

    pl.semaphore_wait(barrier, chips + has_above.astype(jnp.int32) + has_below.astype(jnp.int32))

    @pl.when(has_above)
    def _():
        @pl.loop(0, exposures)
        def _(e):
            for array in (0, 1):
                halo_copy(e, array, False).start()

    @pl.when(has_below)
    def _():
        @pl.loop(0, exposures)
        def _(e):
            for array in (0, 1):
                halo_copy(e, array, True).start()

    @pl.when(jnp.logical_not(has_above))
    def _():
        above[...] = jnp.zeros_like(above)

    @pl.when(jnp.logical_not(has_below))
    def _():
        below[...] = jnp.zeros_like(below)

    lane = lax.broadcasted_iota(jnp.int32, (map_rows, wide), 1)
    row = lax.broadcasted_iota(jnp.int32, (map_rows, wide), 0)
    keep = (lane >= SHIFT) & (lane < SHIFT + columns) & ((row < rows) | has_below)

    flat = maps.reshape(4, exposures * rows * 8, LANES)

    @pl.loop(0, exposures)
    def _(e):
        @pl.when(has_below)
        def _():
            for array in (0, 1):
                halo_copy(e, array, False).wait_recv()

        @pl.when(has_above)
        def _():
            for array in (0, 1):
                halo_copy(e, array, True).wait_recv()

        for place, size, pick in (
            (0, 16, lambda k: above[k, e]),
            (16, rows, lambda k: (sci, inv)[k][e]),
            (16 + rows, rows, lambda k: below[k, e]),
        ):
            inverse = pick(1).astype(jnp.float32)
            rows_in[0, pl.ds(place, size), :] = pick(0).astype(jnp.float32) * inverse
            rows_in[1, pl.ds(place, size), :] = inverse
        ok = usable[e].astype(jnp.float32)
        for which in (0, 1):
            def tap(ref, a):
                value = ref[e, a]
                return value * value if which else value

            filtered = tap(row_taps, 0) * rows_in[which, pl.ds(16 - radius, map_rows), :]
            for a in range(1, taps):
                filtered += tap(row_taps, a) * rows_in[which, pl.ds(16 - radius + a, map_rows), :]
            filtered = jnp.concatenate(
                [filtered, jnp.zeros((map_rows, LANES), jnp.float32)], axis=1
            )
            result = tap(col_taps, 0) * pltpu.roll(filtered, SHIFT + radius, axis=1)
            for b in range(1, taps):
                result += tap(col_taps, b) * pltpu.roll(filtered, SHIFT + radius - b, axis=1)
            result = jnp.where(keep, result, 0.0).astype(jnp.bfloat16).astype(jnp.float32) * ok
            for block in range(blocks + 1):
                for r in range(0, map_rows, 8):
                    tile = result[r : r + 8, block * LANES : (block + 1) * LANES]
                    for later in (0, 1):
                        sub = block - later
                        if sub < 0 or sub >= blocks:
                            continue
                        for at, shift in ((r, sub), (r - half, sub + 4)):
                            if 0 <= at < rows:
                                flat[2 * which + later,
                                     pl.ds((e * rows + at) * 8 + shift, 8, stride=8), :] = tile

    low = lax.broadcasted_iota(jnp.int32, (1, 8, LANES), 1) < 4
    lane8 = lax.broadcasted_iota(jnp.int32, (1, 8, LANES), 2)

    def window(e, velocity, which, start):
        at = e * rows + row_shift[e, velocity] + start
        shift = col_shift[e, velocity] + SHIFT
        here = maps[2 * which, pl.ds(at, 8)]
        after = maps[2 * which + 1, pl.ds(at, 8)]
        mixed = jnp.where(jnp.broadcast_to(lane8 >= shift, here.shape), here, after)
        return pltpu.roll(mixed, LANES - shift, axis=2)

    def put(stage, g, v, start, signal, depth):
        for base, value in (
            (start, jnp.where(low, signal, roll4(depth))),
            (start + half, jnp.where(low, roll4(signal), depth)),
        ):
            for part in range(8 // own):
                owner = base // own + part
                sums[stage][g, owner % 2, owner // 2, v] = value[part * own : (part + 1) * own]

    def get_rows(g, start):
        return jnp.concatenate(
            [
                fluxes[g, (start // own + part) % 2, (start // own + part) // 2]
                for part in range(8 // own)
            ],
            axis=0,
        )

    def pass_on(stage, g):
        near_copy(stage, g).wait_recv()
        pair[stage][g] = sums[stage][g, core] + near[stage][g]
        for j in range(1, chips):
            far_copy(stage, g, j).start()

    def total(stage, g):
        value = pair[stage][g, chip]
        for j in range(1, chips):
            far_copy(stage, g, j).wait_recv()
            value = value + far[stage][g, j - 1]
        return value

    @pl.loop(0, groups)
    def _(g):
        for v in (0, 1):
            for start in range(0, half, 8):
                signal = window(0, 2 * g + v, 0, start)
                depth = window(0, 2 * g + v, 1, start)
                for e in range(1, exposures):
                    signal += window(e, 2 * g + v, 0, start)
                    depth += window(e, 2 * g + v, 1, start)
                put(0, g, v, start, signal, depth)
        near_copy(0, g).start()

        @pl.when(g > 0)
        def _():
            pass_on(0, g - 1)

    pass_on(0, groups - 1)

    @pl.loop(0, groups)
    def _(g):
        whole = total(0, g)
        flux = whole / (roll4(whole) + 1.0)
        fluxes[g, core, chip] = jnp.where(low, flux[0], roll4(flux[1]))
        for j in range(1, chips):
            flux_copy(g, j).start()

        @pl.when(g > 0)
        def _():
            for j in range(1, chips):
                flux_copy(g - 1, j).wait_recv()
            flux_sibling(g - 1).start()

    for j in range(1, chips):
        flux_copy(groups - 1, j).wait_recv()
    flux_sibling(groups - 1).start()

    @pl.loop(0, groups)
    def _(g):
        flux_sibling(g).wait_recv()
        for v in (0, 1):
            for start in range(0, half, 8):
                upper, lower = get_rows(g, start), get_rows(g, start + half)
                if v == 0:
                    flux = jnp.where(low, upper, roll4(lower))
                else:
                    flux = jnp.where(low, roll4(upper), lower)
                signal_sum = jnp.zeros((8, 8, LANES), jnp.float32)
                depth_sum = jnp.zeros((8, 8, LANES), jnp.float32)
                for e in range(exposures):
                    signal = window(e, 2 * g + v, 0, start)
                    depth = window(e, 2 * g + v, 1, start)
                    residual = signal - flux * depth
                    more = depth + 1.0
                    weight = more / (more + residual * residual)
                    signal_sum += weight * signal
                    depth_sum += weight * depth
                put(1, g, v, start, signal_sum, depth_sum)
        near_copy(1, g).start()

        @pl.when(g > 0)
        def _():
            pass_on(1, g - 1)

    pass_on(1, groups - 1)

    @pl.loop(0, groups)
    def _(g):
        whole = total(1, g)
        result = whole / jnp.sqrt(roll4(whole) + 1.0)
        for v in (0, 1):
            out[2 * g + v] = result[v, :, :4, :]

    @pl.loop(0, groups)
    def _(g):
        for stage in (0, 1):
            near_copy(stage, g).wait_send()
            for j in range(1, chips):
                far_copy(stage, g, j).wait_send()
        for j in range(1, chips):
            flux_copy(g, j).wait_send()
        flux_sibling(g).wait_send()

    @pl.when(has_above)
    def _():
        @pl.loop(0, exposures)
        def _(e):
            for array in (0, 1):
                halo_copy(e, array, False).wait_send()

    @pl.when(has_below)
    def _():
        @pl.loop(0, exposures)
        def _(e):
            for array in (0, 1):
                halo_copy(e, array, True).wait_send()


def per_device(count, strips, science, inv_var, psf_rows, psf_cols, row_shift, col_shift, ok):
    exposures, rows, columns = science.shape
    vels, taps = row_shift.shape[1], psf_rows.shape[1]
    chips, own, groups = count // 2, rows // count, vels // 2
    f32, bf16 = jnp.float32, jnp.bfloat16
    dma = lambda *shape: [pltpu.SemaphoreType.DMA(shape)] * 2
    smem = pl.BlockSpec(memory_space=pltpu.SMEM)
    vmem = pl.BlockSpec(memory_space=pltpu.VMEM)
    result = pl.pallas_call(
        functools.partial(kernel, (count, strips, exposures, rows, columns, vels, taps)),
        out_shape=jax.ShapeDtypeStruct((vels, own, columns // LANES, LANES), f32),
        in_specs=[smem] * 5 + [vmem] * 2,
        out_specs=vmem,
        scratch_shapes=[
            pltpu.VMEM((2, exposures, 16, columns), bf16),
            pltpu.VMEM((2, exposures, rows, columns), bf16),
            pltpu.VMEM((2, 16 + 2 * rows, columns), f32),
            pltpu.VMEM((4, exposures * rows, 8, LANES), f32),
            pltpu.VMEM((groups, 2, chips, own, 8, LANES), f32),
            pltpu.VMEM((groups, 2, chips, 2, own, 8, LANES), f32),
            pltpu.VMEM((groups, chips, 2, own, 8, LANES), f32),
            pltpu.VMEM((groups, chips, 2, own, 8, LANES), f32),
            pltpu.VMEM((groups, chips - 1, 2, own, 8, LANES), f32),
            pltpu.VMEM((groups, 2, chips, 2, own, 8, LANES), f32),
            pltpu.VMEM((groups, chips, 2, own, 8, LANES), f32),
            pltpu.VMEM((groups, chips, 2, own, 8, LANES), f32),
            pltpu.VMEM((groups, chips - 1, 2, own, 8, LANES), f32),
            *dma(2, 2, exposures),
            *dma(2, groups),
            *dma(2, groups, chips - 1),
            *dma(groups, chips - 1),
            *dma(groups),
        ],
        compiler_params=pltpu.CompilerParams(
            collective_id=0, has_side_effects=True, vmem_limit_bytes=40 * 1024 * 1024
        ),
    )(psf_rows, psf_cols, row_shift, col_shift, ok, science, inv_var)
    return result.reshape(1, vels, own, columns)


def solution(mesh):
    from jax.sharding import PartitionSpec as P

    in_specs = (
        P(("field", "expo"), "strip", None),
        P(("field", "expo"), "strip", None),
        P(("field", "expo"), None),
        P(("field", "expo"), None),
        P(("field", "expo"), None),
        P(("field", "expo"), None),
        P(("field", "expo")),
    )
    return jax.shard_map(
        functools.partial(per_device, mesh.shape["expo"], mesh.shape["strip"]),
        mesh=mesh,
        in_specs=in_specs,
        out_specs=P("strip", "field", "expo", None),
        check_vma=False,
    )
```

time: 363 us -> 64.2 us (0.18)
  local copies, waits for them, and re-layouts: 198 us -> 5.97 us
  waiting for transfers between devices: 118 us -> 0 us
  Pallas kernels: 0 us -> 57.9 us
  other arithmetic: 23.9 us -> 0 us
  between operations: 13.9 us -> 0.02 us
  starting transfers between devices: 6.46 us -> 0 us
    gather x192 -> x0, local copies, waits for them, and re-layouts: 182 us -> none
    reduce_scatter x2 -> x0, waiting for transfers between devices: 59.6 us -> none  [the longest x1 31.5 us: per_device(): lax.psum_scatter(jnp.stack(robust_signal), 'expo', scatter_dimension=1, t...]
    pallas_call x0 -> x1, Pallas kernels: none -> 57.9 us  [per_device(): pl.pallas_call(functools.partial(kernel, (count, strips, exposures, rows,...]
    psum x1 -> x0, waiting for transfers between devices: 50.5 us -> none  [per_device(): whole_sums = lax.psum((first_sums[:, 0], first_sums[:, 1]), 'expo')]
    ppermute x2 -> x0, waiting for transfers between devices: 8.27 us -> none  [the longest x1 4.14 us: extended_2(): lax.ppermute(head, axis, [((i + 1) % count, i) for i in range(ends)])]
    ppermute x2 -> x0, starting transfers between devices: 6.16 us -> none  [the longest x1 4.87 us: extended_2(): lax.ppermute(tail, axis, [(i, (i + 1) % count) for i in range(ends)])]
    convert_element_type x10 -> x0, other arithmetic: 6.1 us -> none  [the longest x8 5.94 us: cut_all(): jax.vmap(cut_one)(padded, row_shift[:, velocity], col_shift[:, velocity])]
    reduce_sum x9 -> x0, other arithmetic: 4.61 us -> none  [the longest x1 2.73 us: per_device(): jnp.sum(usable * cut_all(velocity), axis=0)]
  transfers between devices with their start and end apart: 5 -> 0, of which waited for: 5 -> 0; matrix products, arithmetic and copies ran while one was open for 3% -> 0% of each run, Pallas kernels for 0% -> 0%
where the time goes in v1:
time: 64.2 us; the launch traced here: 63.9 us
  Pallas kernels  57.9 us (90%)
  local copies, waits for them, and re-layouts  5.97 us (9%)
    pallas_call x1, Pallas kernels, per_device(): pl.pallas_call(functools.partial(kernel, (count, strips, exposures, rows,...  57.9 us
    unnamed x14, local copies, waits for them, and re-layouts  5.3 us

profile of v1, /device:TPU:0, one launch (start us, length us, event | category | flops | bytes accessed | tf_op | source)
XLA Modules:
  0.0 63.9 jit_solution(13946440854254924489)
XLA Ops:
  0.0 0.0 copy-start
  0.0 0.9 %copy-done = bf16[8,32,512]{2,1,0:T(8,128)(2,1)S(1)} copy-done((bf16[8,32,512]{2,1,0:T(8,128)(2,1)S(1)}, bf16[8,32,512]{2,1,0:T(8,128)(2,1)}, u32[]{:S(2)}) %copy-start) | copy-done | bytes 262168
  1.0 0.0 copy-start.1
  1.0 0.9 %copy-done.1 = bf16[8,32,512]{2,1,0:T(8,128)(2,1)S(1)} copy-done((bf16[8,32,512]{2,1,0:T(8,128)(2,1)S(1)}, bf16[8,32,512]{2,1,0:T(8,128)(2,1)}, u32[]{:S(2)}) %copy-start.1) | copy-done | bytes 262168
  1.9 0.0 copy-start.2
  1.9 0.7 %copy-done.2 = f32[8,9]{1,0:T(8,128)S(1)} copy-done((f32[8,9]{1,0:T(8,128)S(1)}, f32[8,9]{1,0:T(8,128)}, u32[]{:S(2)}) %copy-start.2) | copy-done | bytes 312
  2.6 0.0 copy-start.3
  2.6 0.7 %copy-done.3 = f32[8,9]{1,0:T(8,128)S(1)} copy-done((f32[8,9]{1,0:T(8,128)S(1)}, f32[8,9]{1,0:T(8,128)}, u32[]{:S(2)}) %copy-start.3) | copy-done | bytes 312
  3.3 0.0 copy-start.4
  3.3 0.7 %copy-done.4 = s32[8,8]{1,0:T(8,128)S(1)} copy-done((s32[8,8]{1,0:T(8,128)S(1)}, s32[8,8]{1,0:T(8,128)}, u32[]{:S(2)}) %copy-start.4) | copy-done | bytes 280
  4.0 0.0 copy-start.5
  4.0 0.7 %copy-done.5 = s32[8,8]{1,0:T(8,128)S(1)} copy-done((s32[8,8]{1,0:T(8,128)S(1)}, s32[8,8]{1,0:T(8,128)}, u32[]{:S(2)}) %copy-start.5) | copy-done | bytes 280
  4.7 0.0 copy-start.6
  4.7 0.7 %copy-done.6 = s32[8]{0:T(128)S(1)} copy-done((s32[8]{0:T(128)S(1)}, s32[8]{0:T(128)}, u32[]{:S(2)}) %copy-start.6) | copy-done | bytes 56
  5.3 57.9 %shard_map.73 = f32[8,4,4,128]{3,2,1,0:T(4,128)S(1)} custom-call(f32[8,9]{1,0:T(8,128)S(1)} %copy-done.2, f32[8,9]{1,0:T(8,128)S(1)} %copy-done.3, s32[8,8]{1,0:T(8,128)S(1)} %copy-done.4, s32[8,8]{1,0:T(8,128)S(1)} %copy-done.5, s32[8]{0:T(128)S(1)} %copy-done.6, bf16[8,32,512]{2,1,0:T(8,128)(2,1)S(1)} %copy-done, bf16[8,32,512]{2,1,0:T(8,128)(2,1)S(1)} %copy-done.1), custom_call_target="tpu_custom_call" | custom-call | tf_op jit(solution)/shard_map/pallas_call | solution.py:327
  63.2 0.7 %reshape.3 = f32[1,8,4,512]{3,2,1,0:T(4,128)} reshape(f32[8,4,4,128]{3,2,1,0:T(4,128)S(1)} %shard_map.73) | data formatting | bytes 131072 | tf_op jit(solution)/shard_map/reshape | solution.py:356
Async XLA Ops:
  0.0 0.9 %copy-start = (bf16[8,32,512]{2,1,0:T(8,128)(2,1)S(1)}, bf16[8,32,512]{2,1,0:T(8,128)(2,1)}, u32[]{:S(2)}) copy-start(bf16[8,32,512]{2,1,0:T(8,128)(2,1)} %sci.1) | copy-start | bytes 786436
  1.0 0.9 %copy-start.1 = (bf16[8,32,512]{2,1,0:T(8,128)(2,1)S(1)}, bf16[8,32,512]{2,1,0:T(8,128)(2,1)}, u32[]{:S(2)}) copy-start(bf16[8,32,512]{2,1,0:T(8,128)(2,1)} %inv.1) | copy-start | bytes 786436
  1.9 0.7 %copy-start.2 = (f32[8,9]{1,0:T(8,128)S(1)}, f32[8,9]{1,0:T(8,128)}, u32[]{:S(2)}) copy-start(f32[8,9]{1,0:T(8,128)} %row_taps.1) | copy-start | bytes 868
  2.6 0.7 %copy-start.3 = (f32[8,9]{1,0:T(8,128)S(1)}, f32[8,9]{1,0:T(8,128)}, u32[]{:S(2)}) copy-start(f32[8,9]{1,0:T(8,128)} %col_taps.1) | copy-start | bytes 868
  3.3 0.7 %copy-start.4 = (s32[8,8]{1,0:T(8,128)S(1)}, s32[8,8]{1,0:T(8,128)}, u32[]{:S(2)}) copy-start(s32[8,8]{1,0:T(8,128)} %row_shift.1) | copy-start | bytes 772
  4.0 0.7 %copy-start.5 = (s32[8,8]{1,0:T(8,128)S(1)}, s32[8,8]{1,0:T(8,128)}, u32[]{:S(2)}) copy-start(s32[8,8]{1,0:T(8,128)} %col_shift.1) | copy-start | bytes 772
  4.7 0.7 %copy-start.6 = (s32[8]{0:T(128)S(1)}, s32[8]{0:T(128)}, u32[]{:S(2)}) copy-start(s32[8]{0:T(128)} %usable.1) | copy-start | bytes 100

commit v2 on v1

--- a/solution.py
+++ b/solution.py
@@ -17,10 +17,11 @@
 
 def kernel(
     cfg,
-    row_taps, col_taps, row_shift, col_shift, usable, sci, inv,
-    out,
-    above, below, rows_in, maps, fluxes, *rest,
+    *refs,
 ):
+    out, inputs, copied = refs[7], refs[:7], refs[8:15]
+    row_taps, col_taps, row_shift, col_shift, usable, sci, inv = copied
+    (in_s, below, tails, above, edge_out, edges, rows_in, maps, stacks, fluxes, *rest) = refs[15:]
     count, strips, exposures, rows, columns, vels, taps = cfg
     radius = taps // 2
     chips = count // 2
@@ -30,8 +31,11 @@
     groups = vels // 2
     wide = columns + LANES
     map_rows = rows + SHIFT
-    sums, near, pair, far = zip(rest[0:4], rest[4:8])
-    (halo_s, halo_r, near_s, near_r, far_s, far_r, flux_s, flux_r, fsib_s, fsib_r) = rest[8:]
+    sums, near, mine, pair, far = zip(rest[0:5], rest[5:10])
+    (full_s, full_r, edge_s, edge_r, near_s, near_r,
+     far_s, far_r, flux_s, flux_r, fsib_s, fsib_r) = rest[10:]
+    per_tile = 16 // radius
+    tiles = exposures // per_tile
 
     me = lax.axis_index("expo")
     strip = lax.axis_index("strip")
@@ -43,16 +47,18 @@
     def peer(j):
         return (chip + j) % chips
 
-    def halo_copy(e, array, down):
-        source = (sci, inv)[array]
-        if down:
-            src, dst, to = source.at[e, pl.ds(rows - 16, 16)], above.at[array, e], strip + 1
-        else:
-            src, dst, to = source.at[e], below.at[array, e], strip - 1
-        slot = (1 if down else 0, array, e)
-        return pltpu.make_async_remote_copy(
-            src_ref=src, dst_ref=dst, send_sem=halo_s.at[slot], recv_sem=halo_r.at[slot],
-            device_id={"strip": to}, device_id_type=MESH,
+    def full_copy(e, array):
+        return pltpu.make_async_remote_copy(
+            src_ref=(sci, inv)[array].at[e, pl.ds(0, SHIFT)], dst_ref=below.at[array, e],
+            send_sem=full_s.at[array, e], recv_sem=full_r.at[array, e],
+            device_id={"strip": strip - 1}, device_id_type=MESH,
+        )
+
+    def edge_copy(t, array, down):
+        return pltpu.make_async_remote_copy(
+            src_ref=edge_out.at[down, array, t], dst_ref=(tails, above)[down].at[array, t],
+            send_sem=edge_s.at[down, array, t], recv_sem=edge_r.at[down, array, t],
+            device_id={"strip": strip + 1 if down else strip - 1}, device_id_type=MESH,
         )
 
     def near_copy(stage, g):
@@ -84,6 +90,11 @@
             device_id={"expo": sibling}, device_id_type=MESH,
         )
 
+    local = [
+        pltpu.make_async_copy(inputs[k], copied[k], in_s.at[k]) for k in (5, 6, 0, 1, 2, 3, 4)
+    ]
+    for copy in local:
+        copy.start()
     barrier = pltpu.get_barrier_semaphore()
     pl.semaphore_signal(barrier, inc=1, device_id={"expo": sibling}, device_id_type=MESH)
     for j in range(1, chips):
@@ -99,21 +110,39 @@
     def _():
         pl.semaphore_signal(barrier, inc=1, device_id={"strip": strip + 1}, device_id_type=MESH)
 
+    for copy in local[:2]:
+        copy.wait()
+    for array, source in enumerate((sci, inv)):
+        for t in range(tiles):
+            span = range(t * per_tile, (t + 1) * per_tile)
+            for down, at in ((0, SHIFT), (1, rows - radius)):
+                base = at // 16 * 16
+                pieces = [
+                    source[e, base : base + 16, :].astype(jnp.float32)[
+                        at - base : at - base + radius
+                    ]
+                    for e in span
+                ]
+                edge_out[down, array, t] = jnp.concatenate(pieces, axis=0).astype(jnp.bfloat16)
     pl.semaphore_wait(barrier, chips + has_above.astype(jnp.int32) + has_below.astype(jnp.int32))
 
+    @pl.when(has_below)
+    def _():
+        for t in range(tiles):
+            for array in (0, 1):
+                edge_copy(t, array, 1).start()
+
     @pl.when(has_above)
     def _():
-        @pl.loop(0, exposures)
-        def _(e):
-            for array in (0, 1):
-                halo_copy(e, array, False).start()
-
-    @pl.when(has_below)
-    def _():
-        @pl.loop(0, exposures)
-        def _(e):
-            for array in (0, 1):
-                halo_copy(e, array, True).start()
+        @pl.loop(0, tiles)
+        def _(t):
+            for array in (0, 1):
+                edge_copy(t, array, 0).start()
+
+            @pl.loop(0, per_tile)
+            def _(q):
+                for array in (0, 1):
+                    full_copy(t * per_tile + q, array).start()
 
     @pl.when(jnp.logical_not(has_above))
     def _():
@@ -122,29 +151,62 @@
     @pl.when(jnp.logical_not(has_below))
     def _():
         below[...] = jnp.zeros_like(below)
+        tails[...] = jnp.zeros_like(tails)
+
+    stacks[...] = jnp.zeros_like(stacks)
+    for copy in local[2:]:
+        copy.wait()
 
     lane = lax.broadcasted_iota(jnp.int32, (map_rows, wide), 1)
     row = lax.broadcasted_iota(jnp.int32, (map_rows, wide), 0)
     keep = (lane >= SHIFT) & (lane < SHIFT + columns) & ((row < rows) | has_below)
 
+    low = lax.broadcasted_iota(jnp.int32, (1, 8, LANES), 1) < 4
+    lane8 = lax.broadcasted_iota(jnp.int32, (1, 8, LANES), 2)
+
+    def window(e, velocity, which, start):
+        at = e * rows + row_shift[e, velocity] + start
+        shift = col_shift[e, velocity] + SHIFT
+        here = maps[2 * which, pl.ds(at, 8)]
+        after = maps[2 * which + 1, pl.ds(at, 8)]
+        mixed = jnp.where(jnp.broadcast_to(lane8 >= shift, here.shape), here, after)
+        return pltpu.roll(mixed, (LANES - shift) & (LANES - 1), axis=2)
+
     flat = maps.reshape(4, exposures * rows * 8, LANES)
 
     @pl.loop(0, exposures)
     def _(e):
+        tile_now, place_in_tile = e // per_tile, e % per_tile
+
+        @pl.when(place_in_tile == 0)
+        def _():
+            @pl.when(has_below)
+            def _():
+                for array in (0, 1):
+                    edge_copy(tile_now, array, 0).wait_recv()
+
+            @pl.when(has_above)
+            def _():
+                for array in (0, 1):
+                    edge_copy(tile_now, array, 1).wait_recv()
+
+            for down, source in enumerate((tails, above)):
+                for array in (0, 1):
+                    tile = source[array, tile_now].astype(jnp.float32)
+                    for q in range(per_tile):
+                        piece = tile[q * radius : (q + 1) * radius]
+                        edges[down, array, q] = jnp.concatenate([piece] * (8 // radius), axis=0)
+
         @pl.when(has_below)
         def _():
             for array in (0, 1):
-                halo_copy(e, array, False).wait_recv()
-
-        @pl.when(has_above)
-        def _():
-            for array in (0, 1):
-                halo_copy(e, array, True).wait_recv()
+                full_copy(e, array).wait_recv()
 
         for place, size, pick in (
-            (0, 16, lambda k: above[k, e]),
-            (16, rows, lambda k: (sci, inv)[k][e]),
-            (16 + rows, rows, lambda k: below[k, e]),
+            (0, 8, lambda k: edges[1, k, place_in_tile]),
+            (8, rows, lambda k: (sci, inv)[k][e]),
+            (8 + rows, SHIFT, lambda k: below[k, e]),
+            (8 + rows + SHIFT, 8, lambda k: edges[0, k, place_in_tile]),
         ):
             inverse = pick(1).astype(jnp.float32)
             rows_in[0, pl.ds(place, size), :] = pick(0).astype(jnp.float32) * inverse
@@ -155,9 +217,9 @@
                 value = ref[e, a]
                 return value * value if which else value
 
-            filtered = tap(row_taps, 0) * rows_in[which, pl.ds(16 - radius, map_rows), :]
+            filtered = tap(row_taps, 0) * rows_in[which, pl.ds(8 - radius, map_rows), :]
             for a in range(1, taps):
-                filtered += tap(row_taps, a) * rows_in[which, pl.ds(16 - radius + a, map_rows), :]
+                filtered += tap(row_taps, a) * rows_in[which, pl.ds(8 - radius + a, map_rows), :]
             filtered = jnp.concatenate(
                 [filtered, jnp.zeros((map_rows, LANES), jnp.float32)], axis=1
             )
@@ -177,16 +239,11 @@
                                 flat[2 * which + later,
                                      pl.ds((e * rows + at) * 8 + shift, 8, stride=8), :] = tile
 
-    low = lax.broadcasted_iota(jnp.int32, (1, 8, LANES), 1) < 4
-    lane8 = lax.broadcasted_iota(jnp.int32, (1, 8, LANES), 2)
-
-    def window(e, velocity, which, start):
-        at = e * rows + row_shift[e, velocity] + start
-        shift = col_shift[e, velocity] + SHIFT
-        here = maps[2 * which, pl.ds(at, 8)]
-        after = maps[2 * which + 1, pl.ds(at, 8)]
-        mixed = jnp.where(jnp.broadcast_to(lane8 >= shift, here.shape), here, after)
-        return pltpu.roll(mixed, LANES - shift, axis=2)
+        @pl.loop(0, vels)
+        def _(velocity):
+            for which in (0, 1):
+                for start in range(0, half, 8):
+                    stacks[velocity, which, pl.ds(start, 8)] += window(e, velocity, which, start)
 
     def put(stage, g, v, start, signal, depth):
         for base, value in (
@@ -208,27 +265,28 @@
 
     def pass_on(stage, g):
         near_copy(stage, g).wait_recv()
-        pair[stage][g] = sums[stage][g, core] + near[stage][g]
+        mine[stage][g] = sums[stage][g, core, chip] + near[stage][g, chip]
         for j in range(1, chips):
+            there = peer(j)
+            both = sums[stage][g, core, there] + near[stage][g, there]
+            pair[stage][g, there] = both.reshape(2, own * 8, LANES).astype(jnp.bfloat16)
             far_copy(stage, g, j).start()
 
     def total(stage, g):
-        value = pair[stage][g, chip]
+        value = mine[stage][g]
         for j in range(1, chips):
             far_copy(stage, g, j).wait_recv()
-            value = value + far[stage][g, j - 1]
+            value = value + far[stage][g, j - 1].astype(jnp.float32).reshape(value.shape)
         return value
 
     @pl.loop(0, groups)
     def _(g):
         for v in (0, 1):
             for start in range(0, half, 8):
-                signal = window(0, 2 * g + v, 0, start)
-                depth = window(0, 2 * g + v, 1, start)
-                for e in range(1, exposures):
-                    signal += window(e, 2 * g + v, 0, start)
-                    depth += window(e, 2 * g + v, 1, start)
-                put(0, g, v, start, signal, depth)
+                put(
+                    0, g, v, start,
+                    stacks[2 * g + v, 0, pl.ds(start, 8)], stacks[2 * g + v, 1, pl.ds(start, 8)],
+                )
         near_copy(0, g).start()
 
         @pl.when(g > 0)
@@ -301,19 +359,22 @@
             flux_copy(g, j).wait_send()
         flux_sibling(g).wait_send()
 
+    @pl.when(has_below)
+    def _():
+        for t in range(tiles):
+            for array in (0, 1):
+                edge_copy(t, array, 1).wait_send()
+
     @pl.when(has_above)
     def _():
+        for t in range(tiles):
+            for array in (0, 1):
+                edge_copy(t, array, 0).wait_send()
+
         @pl.loop(0, exposures)
         def _(e):
             for array in (0, 1):
-                halo_copy(e, array, False).wait_send()
-
-    @pl.when(has_below)
-    def _():
-        @pl.loop(0, exposures)
-        def _(e):
-            for array in (0, 1):
-                halo_copy(e, array, True).wait_send()
+                full_copy(e, array).wait_send()
 
 
 def per_device(count, strips, science, inv_var, psf_rows, psf_cols, row_shift, col_shift, ok):
@@ -322,35 +383,49 @@
     chips, own, groups = count // 2, rows // count, vels // 2
     f32, bf16 = jnp.float32, jnp.bfloat16
     dma = lambda *shape: [pltpu.SemaphoreType.DMA(shape)] * 2
-    smem = pl.BlockSpec(memory_space=pltpu.SMEM)
-    vmem = pl.BlockSpec(memory_space=pltpu.VMEM)
+    radius = taps // 2
+    tiles = exposures * radius // 16
+    stage = [
+        pltpu.VMEM((groups, 2, chips, 2, own, 8, LANES), f32),
+        pltpu.VMEM((groups, chips, 2, own, 8, LANES), f32),
+        pltpu.VMEM((groups, 2, own, 8, LANES), f32),
+        pltpu.VMEM((groups, chips, 2, own * 8, LANES), bf16),
+        pltpu.VMEM((groups, chips - 1, 2, own * 8, LANES), bf16),
+    ]
     result = pl.pallas_call(
         functools.partial(kernel, (count, strips, exposures, rows, columns, vels, taps)),
         out_shape=jax.ShapeDtypeStruct((vels, own, columns // LANES, LANES), f32),
-        in_specs=[smem] * 5 + [vmem] * 2,
-        out_specs=vmem,
+        in_specs=[pl.BlockSpec(memory_space=pl.ANY)] * 7,
+        out_specs=pl.BlockSpec(memory_space=pltpu.VMEM),
         scratch_shapes=[
-            pltpu.VMEM((2, exposures, 16, columns), bf16),
-            pltpu.VMEM((2, exposures, rows, columns), bf16),
-            pltpu.VMEM((2, 16 + 2 * rows, columns), f32),
+            pltpu.SMEM(psf_rows.shape, f32),
+            pltpu.SMEM(psf_cols.shape, f32),
+            pltpu.SMEM(row_shift.shape, jnp.int32),
+            pltpu.SMEM(col_shift.shape, jnp.int32),
+            pltpu.SMEM(ok.shape, jnp.int32),
+            pltpu.VMEM(science.shape, bf16),
+            pltpu.VMEM(science.shape, bf16),
+            pltpu.SemaphoreType.DMA((7,)),
+            pltpu.VMEM((2, exposures, SHIFT, columns), bf16),
+            pltpu.VMEM((2, tiles, 16, columns), bf16),
+            pltpu.VMEM((2, tiles, 16, columns), bf16),
+            pltpu.VMEM((2, 2, tiles, 16, columns), bf16),
+            pltpu.VMEM((2, 2, 16 // radius, 8, columns), f32),
+            pltpu.VMEM((2, 16 + rows + SHIFT, columns), f32),
             pltpu.VMEM((4, exposures * rows, 8, LANES), f32),
+            pltpu.VMEM((vels, 2, rows // 2, 8, LANES), f32),
             pltpu.VMEM((groups, 2, chips, own, 8, LANES), f32),
-            pltpu.VMEM((groups, 2, chips, 2, own, 8, LANES), f32),
-            pltpu.VMEM((groups, chips, 2, own, 8, LANES), f32),
-            pltpu.VMEM((groups, chips, 2, own, 8, LANES), f32),
-            pltpu.VMEM((groups, chips - 1, 2, own, 8, LANES), f32),
-            pltpu.VMEM((groups, 2, chips, 2, own, 8, LANES), f32),
-            pltpu.VMEM((groups, chips, 2, own, 8, LANES), f32),
-            pltpu.VMEM((groups, chips, 2, own, 8, LANES), f32),
-            pltpu.VMEM((groups, chips - 1, 2, own, 8, LANES), f32),
-            *dma(2, 2, exposures),
+            *stage,
+            *stage,
+            *dma(2, exposures),
+            *dma(2, 2, tiles),
             *dma(2, groups),
             *dma(2, groups, chips - 1),
             *dma(groups, chips - 1),
             *dma(groups),
         ],
         compiler_params=pltpu.CompilerParams(
-            collective_id=0, has_side_effects=True, vmem_limit_bytes=40 * 1024 * 1024
+            collective_id=0, has_side_effects=True, vmem_limit_bytes=60 * 1024 * 1024
         ),
     )(psf_rows, psf_cols, row_shift, col_shift, ok, science, inv_var)
     return result.reshape(1, vels, own, columns)

time: 64.2 us -> 50.7 us (0.79)
  Pallas kernels: 57.9 us -> 49 us
  local copies, waits for them, and re-layouts: 5.97 us -> 1.51 us
    pallas_call x1, Pallas kernels: 57.9 us -> 49 us  [per_device(): pl.pallas_call(functools.partial(kernel, (count, strips, exposures, rows,...]
    unnamed x14 -> x0, local copies, waits for them, and re-layouts: 5.3 us -> none
    reshape x1, local copies, waits for them, and re-layouts: 0.67 us -> 1.51 us  [per_device(): return result.reshape(1, vels, own, columns)]
where the time goes in v2:
time: 50.7 us; the launch traced here: 50.5 us
  Pallas kernels  49 us (97%)
  local copies, waits for them, and re-layouts  1.51 us (3%)
    pallas_call x1, Pallas kernels, per_device(): pl.pallas_call(functools.partial(kernel, (count, strips, exposures, rows,...  49 us
    reshape x1, local copies, waits for them, and re-layouts, per_device(): return result.reshape(1, vels, own, columns)  1.51 us

profile of v2, /device:TPU:0, one launch (start us, length us, event | category | flops | bytes accessed | tf_op | source)
XLA Modules:
  0.0 50.5 jit_solution(11193939332340731614)
XLA Ops:
  0.0 49.0 %shard_map.73 = f32[8,4,4,128]{3,2,1,0:T(4,128)} custom-call(f32[8,9]{1,0:T(8,128)} %refs_0_.1, f32[8,9]{1,0:T(8,128)} %refs_1_.1, s32[8,8]{1,0:T(8,128)} %refs_2_.1, s32[8,8]{1,0:T(8,128)} %refs_3_.1, s32[8]{0:T(128)} %refs_4_.1, bf16[8,32,512]{2,1,0:T(8,128)(2,1)} %refs_5_.1, bf16[8,32,512]{2,1,0:T(8,128)(2,1)} %refs_6_.1), custom_call_target="tpu_custom_call" | custom-call | tf_op jit(solution)/shard_map/pallas_call | solution.py:395
  49.0 1.5 %reshape.3 = f32[1,8,4,512]{3,2,1,0:T(4,128)} reshape(f32[8,4,4,128]{3,2,1,0:T(4,128)} %shard_map.73) | data formatting | bytes 131072 | tf_op jit(solution)/shard_map/reshape | solution.py:431

commit v3 on v2

--- a/solution.py
+++ b/solution.py
@@ -1,4 +1,5 @@
 import functools
+import math
 
 import jax
 import jax.numpy as jnp
@@ -9,6 +10,21 @@
 SHIFT = 16
 LANES = 128
 MESH = pl.DeviceIdType.MESH
+
+
+LEAST = 2.0 ** -20
+STEPS = 32700.0
+
+
+def to_code(x, steps):
+    level = jnp.log(1.0 + jnp.abs(x) * (1.0 / LEAST)) * steps + 0.5
+    return jnp.where(x < 0, -level, level).astype(jnp.int32).astype(jnp.int16)
+
+
+def from_code(code, steps):
+    level = code.astype(jnp.int32).astype(jnp.float32)
+    size = (jnp.exp(jnp.abs(level) * (1.0 / steps)) - 1.0) * LEAST
+    return jnp.where(level < 0, -size, size)
 
 
 def roll4(x):
@@ -21,7 +37,7 @@
 ):
     out, inputs, copied = refs[7], refs[:7], refs[8:15]
     row_taps, col_taps, row_shift, col_shift, usable, sci, inv = copied
-    (in_s, below, tails, above, edge_out, edges, rows_in, maps, stacks, fluxes, *rest) = refs[15:]
+    (in_s, below, tails, above, edge_out, edges, rows_in, maps, stacks, fluxes, final, *rest) = refs[15:]
     count, strips, exposures, rows, columns, vels, taps = cfg
     radius = taps // 2
     chips = count // 2
@@ -35,6 +51,8 @@
     (full_s, full_r, edge_s, edge_r, near_s, near_r,
      far_s, far_r, flux_s, flux_r, fsib_s, fsib_r) = rest[10:]
     per_tile = 16 // radius
+    most = 2.0 * exposures * 24.0 * taps * taps * 1.01
+    steps = STEPS / math.log(1.0 + most / LEAST)
     tiles = exposures // per_tile
 
     me = lax.axis_index("expo")
@@ -257,11 +275,13 @@
     def get_rows(g, start):
         return jnp.concatenate(
             [
-                fluxes[g, (start // own + part) % 2, (start // own + part) // 2]
+                from_code(
+                    fluxes[g, (start // own + part) % 2, (start // own + part) // 2], steps
+                )
                 for part in range(8 // own)
             ],
             axis=0,
-        )
+        ).reshape(8, 8, LANES)
 
     def pass_on(stage, g):
         near_copy(stage, g).wait_recv()
@@ -269,14 +289,14 @@
         for j in range(1, chips):
             there = peer(j)
             both = sums[stage][g, core, there] + near[stage][g, there]
-            pair[stage][g, there] = both.reshape(2, own * 8, LANES).astype(jnp.bfloat16)
+            pair[stage][g, there] = to_code(both.reshape(2, own * 8, LANES), steps)
             far_copy(stage, g, j).start()
 
     def total(stage, g):
         value = mine[stage][g]
         for j in range(1, chips):
             far_copy(stage, g, j).wait_recv()
-            value = value + far[stage][g, j - 1].astype(jnp.float32).reshape(value.shape)
+            value = value + from_code(far[stage][g, j - 1], steps).reshape(value.shape)
         return value
 
     @pl.loop(0, groups)
@@ -295,30 +315,24 @@
 
     pass_on(0, groups - 1)
 
-    @pl.loop(0, groups)
-    def _(g):
+    def spread_flux(g):
         whole = total(0, g)
         flux = whole / (roll4(whole) + 1.0)
-        fluxes[g, core, chip] = jnp.where(low, flux[0], roll4(flux[1]))
+        flux = jnp.where(low, flux[0], roll4(flux[1])).reshape(own * 8, LANES)
+        fluxes[g, core, chip] = to_code(flux, steps)
         for j in range(1, chips):
             flux_copy(g, j).start()
 
-        @pl.when(g > 0)
-        def _():
-            for j in range(1, chips):
-                flux_copy(g - 1, j).wait_recv()
-            flux_sibling(g - 1).start()
-
-    for j in range(1, chips):
-        flux_copy(groups - 1, j).wait_recv()
-    flux_sibling(groups - 1).start()
-
-    @pl.loop(0, groups)
-    def _(g):
+    def share_flux(g):
+        for j in range(1, chips):
+            flux_copy(g, j).wait_recv()
+        flux_sibling(g).start()
+
+    def reweight(g):
         flux_sibling(g).wait_recv()
-        for v in (0, 1):
-            for start in range(0, half, 8):
-                upper, lower = get_rows(g, start), get_rows(g, start + half)
+        for start in range(0, half, 8):
+            upper, lower = get_rows(g, start), get_rows(g, start + half)
+            for v in (0, 1):
                 if v == 0:
                     flux = jnp.where(low, upper, roll4(lower))
                 else:
@@ -336,18 +350,34 @@
                 put(1, g, v, start, signal_sum, depth_sum)
         near_copy(1, g).start()
 
-        @pl.when(g > 0)
-        def _():
-            pass_on(1, g - 1)
-
-    pass_on(1, groups - 1)
+    @pl.loop(0, groups + 3)
+    def _(i):
+        @pl.when(i < groups)
+        def _():
+            spread_flux(i)
+
+        @pl.when((i >= 1) & (i < groups + 1))
+        def _():
+            share_flux(i - 1)
+
+        @pl.when(i >= 3)
+        def _():
+            pass_on(1, i - 3)
+
+        @pl.when((i >= 2) & (i < groups + 2))
+        def _():
+            reweight(i - 2)
 
     @pl.loop(0, groups)
     def _(g):
         whole = total(1, g)
         result = whole / jnp.sqrt(roll4(whole) + 1.0)
+        final[...] = result.reshape(2 * own * 8, LANES)
         for v in (0, 1):
-            out[2 * g + v] = result[v, :, :4, :]
+            for block in range(blocks):
+                out[2 * g + v, :, block * LANES : (block + 1) * LANES] = final[
+                    pl.ds(v * own * 8 + block, own, stride=8), :
+                ]
 
     @pl.loop(0, groups)
     def _(g):
@@ -389,12 +419,12 @@
         pltpu.VMEM((groups, 2, chips, 2, own, 8, LANES), f32),
         pltpu.VMEM((groups, chips, 2, own, 8, LANES), f32),
         pltpu.VMEM((groups, 2, own, 8, LANES), f32),
-        pltpu.VMEM((groups, chips, 2, own * 8, LANES), bf16),
-        pltpu.VMEM((groups, chips - 1, 2, own * 8, LANES), bf16),
+        pltpu.VMEM((groups, chips, 2, own * 8, LANES), jnp.int16),
+        pltpu.VMEM((groups, chips - 1, 2, own * 8, LANES), jnp.int16),
     ]
     result = pl.pallas_call(
         functools.partial(kernel, (count, strips, exposures, rows, columns, vels, taps)),
-        out_shape=jax.ShapeDtypeStruct((vels, own, columns // LANES, LANES), f32),
+        out_shape=jax.ShapeDtypeStruct((vels, own, columns), f32),
         in_specs=[pl.BlockSpec(memory_space=pl.ANY)] * 7,
         out_specs=pl.BlockSpec(memory_space=pltpu.VMEM),
         scratch_shapes=[
@@ -414,7 +444,8 @@
             pltpu.VMEM((2, 16 + rows + SHIFT, columns), f32),
             pltpu.VMEM((4, exposures * rows, 8, LANES), f32),
             pltpu.VMEM((vels, 2, rows // 2, 8, LANES), f32),
-            pltpu.VMEM((groups, 2, chips, own, 8, LANES), f32),
+            pltpu.VMEM((groups, 2, chips, own * 8, LANES), jnp.int16),
+            pltpu.VMEM((2 * own * 8, LANES), f32),
             *stage,
             *stage,
             *dma(2, exposures),

time: 50.7 us -> 48.1 us (0.949)
  Pallas kernels: 49 us -> 46.5 us
    pallas_call x1, Pallas kernels: 49 us -> 46.5 us  [per_device(): pl.pallas_call(functools.partial(kernel, (count, strips, exposures, rows,...]
    reshape x1 -> x0, local copies, waits for them, and re-layouts: 1.51 us -> none  [per_device(): return result.reshape(1, vels, own, columns)]
    unnamed x0 -> x1, local copies, waits for them, and re-layouts: none -> 1.47 us
where the time goes in v3:
time: 48.1 us; the launch traced here: 47.9 us
  Pallas kernels  46.5 us (97%)
  local copies, waits for them, and re-layouts  1.47 us (3%)
    pallas_call x1, Pallas kernels, per_device(): pl.pallas_call(functools.partial(kernel, (count, strips, exposures, rows,...  46.5 us
    unnamed x1, local copies, waits for them, and re-layouts  1.47 us

profile of v3, /device:TPU:0, one launch (start us, length us, event | category | flops | bytes accessed | tf_op | source)
XLA Modules:
  0.0 47.9 jit_solution(4872693304134495157)
XLA Ops:
  0.0 46.5 %shard_map.73 = f32[8,4,512]{2,1,0:T(4,128)} custom-call(f32[8,9]{1,0:T(8,128)} %refs_0_.1, f32[8,9]{1,0:T(8,128)} %refs_1_.1, s32[8,8]{1,0:T(8,128)} %refs_2_.1, s32[8,8]{1,0:T(8,128)} %refs_3_.1, s32[8]{0:T(128)} %refs_4_.1, bf16[8,32,512]{2,1,0:T(8,128)(2,1)} %refs_5_.1, bf16[8,32,512]{2,1,0:T(8,128)(2,1)} %refs_6_.1), custom_call_target="tpu_custom_call" | custom-call | tf_op jit(solution)/shard_map/pallas_call | solution.py:425
  46.5 1.5 %copy.9 = f32[1,8,4,512]{3,2,1,0:T(4,128)} copy(f32[1,8,4,512]{3,2,1,0:T(4,128)} %bitcast.1) | data formatting | bytes 131072

commit v4 on v3

--- a/solution.py
+++ b/solution.py
@@ -257,8 +257,7 @@
                                 flat[2 * which + later,
                                      pl.ds((e * rows + at) * 8 + shift, 8, stride=8), :] = tile
 
-        @pl.loop(0, vels)
-        def _(velocity):
+        for velocity in range(vels):
             for which in (0, 1):
                 for start in range(0, half, 8):
                     stacks[velocity, which, pl.ds(start, 8)] += window(e, velocity, which, start)
@@ -344,7 +343,9 @@
                     depth = window(e, 2 * g + v, 1, start)
                     residual = signal - flux * depth
                     more = depth + 1.0
-                    weight = more / (more + residual * residual)
+                    bottom = more + residual * residual
+                    guess = pl.reciprocal(bottom, approx=True)
+                    weight = more * (guess * (2.0 - bottom * guess))
                     signal_sum += weight * signal
                     depth_sum += weight * depth
                 put(1, g, v, start, signal_sum, depth_sum)

time: 48.1 us -> 44.3 us (0.921)
  Pallas kernels: 46.5 us -> 42.6 us
    pallas_call x1, Pallas kernels: 46.5 us -> 42.6 us  [per_device(): pl.pallas_call(functools.partial(kernel, (count, strips, exposures, rows,...]
where the time goes in v4:
time: 44.3 us; the launch traced here: 44.1 us
  Pallas kernels  42.6 us (96%)
  local copies, waits for them, and re-layouts  1.47 us (3%)
    pallas_call x1, Pallas kernels, per_device(): pl.pallas_call(functools.partial(kernel, (count, strips, exposures, rows,...  42.6 us
    unnamed x1, local copies, waits for them, and re-layouts  1.47 us

profile of v4, /device:TPU:0, one launch (start us, length us, event | category | flops | bytes accessed | tf_op | source)
XLA Modules:
  0.0 44.1 jit_solution(4232010295601587289)
XLA Ops:
  0.0 42.6 %shard_map.73 = f32[8,4,512]{2,1,0:T(4,128)} custom-call(f32[8,9]{1,0:T(8,128)} %refs_0_.1, f32[8,9]{1,0:T(8,128)} %refs_1_.1, s32[8,8]{1,0:T(8,128)} %refs_2_.1, s32[8,8]{1,0:T(8,128)} %refs_3_.1, s32[8]{0:T(128)} %refs_4_.1, bf16[8,32,512]{2,1,0:T(8,128)(2,1)} %refs_5_.1, bf16[8,32,512]{2,1,0:T(8,128)(2,1)} %refs_6_.1), custom_call_target="tpu_custom_call" | custom-call | tf_op jit(solution)/shard_map/pallas_call | solution.py:426
  42.6 1.5 %copy.9 = f32[1,8,4,512]{3,2,1,0:T(4,128)} copy(f32[1,8,4,512]{3,2,1,0:T(4,128)} %bitcast.1) | data formatting | bytes 131072

commit v5 on v4

--- a/solution.py
+++ b/solution.py
@@ -37,7 +37,7 @@
 ):
     out, inputs, copied = refs[7], refs[:7], refs[8:15]
     row_taps, col_taps, row_shift, col_shift, usable, sci, inv = copied
-    (in_s, below, tails, above, edge_out, edges, rows_in, maps, stacks, fluxes, final, *rest) = refs[15:]
+    (in_s, below, tails, above, edge_out, edges, raw, maps, stacks, fluxes, final, *rest) = refs[15:]
     count, strips, exposures, rows, columns, vels, taps = cfg
     radius = taps // 2
     chips = count // 2
@@ -45,8 +45,7 @@
     half = rows // 2
     blocks = columns // LANES
     groups = vels // 2
-    wide = columns + LANES
-    map_rows = rows + SHIFT
+    apart = (rows + SHIFT) // 2
     sums, near, mine, pair, far = zip(rest[0:5], rest[5:10])
     (full_s, full_r, edge_s, edge_r, near_s, near_r,
      far_s, far_r, flux_s, flux_r, fsib_s, fsib_r) = rest[10:]
@@ -175,22 +174,30 @@
     for copy in local[2:]:
         copy.wait()
 
-    lane = lax.broadcasted_iota(jnp.int32, (map_rows, wide), 1)
-    row = lax.broadcasted_iota(jnp.int32, (map_rows, wide), 0)
-    keep = (lane >= SHIFT) & (lane < SHIFT + columns) & ((row < rows) | has_below)
-
-    low = lax.broadcasted_iota(jnp.int32, (1, 8, LANES), 1) < 4
-    lane8 = lax.broadcasted_iota(jnp.int32, (1, 8, LANES), 2)
+    sub = lax.broadcasted_iota(jnp.int32, (1, 8, LANES), 1)
+    lane = lax.broadcasted_iota(jnp.int32, (1, 8, LANES), 2)
+    low = sub < 4
+    first_block, last_block = sub % 4 == 0, sub % 4 == 3
+    span = exposures * rows
+
+    def choose(mask, x, y):
+        return jnp.where(jnp.broadcast_to(mask, x.shape), x, y)
+
+    def next_blocks(x):
+        return choose(last_block, jnp.zeros_like(x), pltpu.roll(x, 7, axis=1))
+
+    def previous_blocks(x):
+        return choose(first_block, jnp.zeros_like(x), pltpu.roll(x, 1, axis=1))
 
     def window(e, velocity, which, start):
-        at = e * rows + row_shift[e, velocity] + start
-        shift = col_shift[e, velocity] + SHIFT
-        here = maps[2 * which, pl.ds(at, 8)]
-        after = maps[2 * which + 1, pl.ds(at, 8)]
-        mixed = jnp.where(jnp.broadcast_to(lane8 >= shift, here.shape), here, after)
-        return pltpu.roll(mixed, (LANES - shift) & (LANES - 1), axis=2)
-
-    flat = maps.reshape(4, exposures * rows * 8, LANES)
+        shift = col_shift[e, velocity]
+        left = jnp.where(shift < 0, 0, span) + e * rows + row_shift[e, velocity] + start
+        here = maps[which, pl.ds(left, 8)]
+        after = maps[which, pl.ds(left + span, 8)]
+        mixed = choose(lane >= (shift & (LANES - 1)), here, after)
+        return pltpu.roll(mixed, (-shift) & (LANES - 1), axis=2)
+
+    raw_rows = raw.reshape(2, raw.shape[1] * 8, LANES)
 
     @pl.loop(0, exposures)
     def _(e):
@@ -220,42 +227,55 @@
             for array in (0, 1):
                 full_copy(e, array).wait_recv()
 
-        for place, size, pick in (
-            (0, 8, lambda k: edges[1, k, place_in_tile]),
-            (8, rows, lambda k: (sci, inv)[k][e]),
-            (8 + rows, SHIFT, lambda k: below[k, e]),
-            (8 + rows + SHIFT, 8, lambda k: edges[0, k, place_in_tile]),
+        for first, pick in (
+            (-8, lambda k: edges[1, k, place_in_tile]),
+            *((r, lambda k, r=r: (sci, inv)[k][e, r : r + 16, :]) for r in range(0, rows, 16)),
+            (rows, lambda k: below[k, e]),
+            (rows + SHIFT, lambda k: edges[0, k, place_in_tile]),
         ):
             inverse = pick(1).astype(jnp.float32)
-            rows_in[0, pl.ds(place, size), :] = pick(0).astype(jnp.float32) * inverse
-            rows_in[1, pl.ds(place, size), :] = inverse
+            weighted = pick(0).astype(jnp.float32) * inverse
+            for which, value in enumerate((weighted, inverse)):
+                for r in range(first, first + value.shape[0], 8):
+                    for at, shift in ((r + 8, 0), (r + 8 - apart, 4)):
+                        if 0 <= at <= apart + 8:
+                            for block in range(blocks):
+                                raw_rows[
+                                    which, pl.ds(at * 8 + shift + block, 8, stride=8), :
+                                ] = value[
+                                    r - first : r - first + 8,
+                                    block * LANES : (block + 1) * LANES,
+                                ]
         ok = usable[e].astype(jnp.float32)
+        ok_last = jnp.where(low, ok, jnp.where(has_below, ok, 0.0))
         for which in (0, 1):
             def tap(ref, a):
                 value = ref[e, a]
                 return value * value if which else value
 
-            filtered = tap(row_taps, 0) * rows_in[which, pl.ds(8 - radius, map_rows), :]
+            filtered = tap(row_taps, 0) * raw[which, pl.ds(8 - radius, apart)]
             for a in range(1, taps):
-                filtered += tap(row_taps, a) * rows_in[which, pl.ds(8 - radius + a, map_rows), :]
-            filtered = jnp.concatenate(
-                [filtered, jnp.zeros((map_rows, LANES), jnp.float32)], axis=1
+                filtered += tap(row_taps, a) * raw[which, pl.ds(8 - radius + a, apart)]
+            after, before = next_blocks(filtered), previous_blocks(filtered)
+            result = tap(col_taps, radius) * filtered
+            for d in range(1, radius + 1):
+                right = pltpu.roll(choose(lane >= d, filtered, after), LANES - d, axis=2)
+                left = pltpu.roll(choose(lane >= LANES - d, before, filtered), d, axis=2)
+                result += tap(col_taps, radius + d) * right + tap(col_taps, radius - d) * left
+            result = result.astype(jnp.bfloat16).astype(jnp.float32)
+            inside = rows - apart
+            result = jnp.concatenate([result[:inside] * ok, result[inside:] * ok_last], axis=0)
+            step = apart - half
+            table = jnp.concatenate(
+                [
+                    choose(low, result[:step], roll4(result[half:])),
+                    choose(low, result[step:], result[:half]),
+                    choose(low, roll4(result[:inside]), result[half : half + inside]),
+                ],
+                axis=0,
             )
-            result = tap(col_taps, 0) * pltpu.roll(filtered, SHIFT + radius, axis=1)
-            for b in range(1, taps):
-                result += tap(col_taps, b) * pltpu.roll(filtered, SHIFT + radius - b, axis=1)
-            result = jnp.where(keep, result, 0.0).astype(jnp.bfloat16).astype(jnp.float32) * ok
-            for block in range(blocks + 1):
-                for r in range(0, map_rows, 8):
-                    tile = result[r : r + 8, block * LANES : (block + 1) * LANES]
-                    for later in (0, 1):
-                        sub = block - later
-                        if sub < 0 or sub >= blocks:
-                            continue
-                        for at, shift in ((r, sub), (r - half, sub + 4)):
-                            if 0 <= at < rows:
-                                flat[2 * which + later,
-                                     pl.ds((e * rows + at) * 8 + shift, 8, stride=8), :] = tile
+            for copy, value in enumerate((previous_blocks(table), table, next_blocks(table))):
+                maps[which, pl.ds(copy * span + e * rows, rows)] = value
 
         for velocity in range(vels):
             for which in (0, 1):
@@ -442,8 +462,8 @@
             pltpu.VMEM((2, tiles, 16, columns), bf16),
             pltpu.VMEM((2, 2, tiles, 16, columns), bf16),
             pltpu.VMEM((2, 2, 16 // radius, 8, columns), f32),
-            pltpu.VMEM((2, 16 + rows + SHIFT, columns), f32),
-            pltpu.VMEM((4, exposures * rows, 8, LANES), f32),
+            pltpu.VMEM((2, (rows + SHIFT) // 2 + 16, 8, LANES), f32),
+            pltpu.VMEM((2, 3 * exposures * rows, 8, LANES), f32),
             pltpu.VMEM((vels, 2, rows // 2, 8, LANES), f32),
             pltpu.VMEM((groups, 2, chips, own * 8, LANES), jnp.int16),
             pltpu.VMEM((2 * own * 8, LANES), f32),

time: 44.3 us -> 42.9 us (0.968)
  Pallas kernels: 42.6 us -> 41.2 us
    pallas_call x1, Pallas kernels: 42.6 us -> 41.2 us  [per_device(): pl.pallas_call(functools.partial(kernel, (count, strips, exposures, rows,...]
where the time goes in v5:
time: 42.9 us; the launch traced here: 42.7 us
  Pallas kernels  41.2 us (96%)
  local copies, waits for them, and re-layouts  1.47 us (3%)
    pallas_call x1, Pallas kernels, per_device(): pl.pallas_call(functools.partial(kernel, (count, strips, exposures, rows,...  41.2 us
    unnamed x1, local copies, waits for them, and re-layouts  1.47 us

profile of v5, /device:TPU:0, one launch (start us, length us, event | category | flops | bytes accessed | tf_op | source)
XLA Modules:
  0.0 42.7 jit_solution(2296710655609616881)
XLA Ops:
  0.0 41.2 %shard_map.73 = f32[8,4,512]{2,1,0:T(4,128)} custom-call(f32[8,9]{1,0:T(8,128)} %refs_0_.1, f32[8,9]{1,0:T(8,128)} %refs_1_.1, s32[8,8]{1,0:T(8,128)} %refs_2_.1, s32[8,8]{1,0:T(8,128)} %refs_3_.1, s32[8]{0:T(128)} %refs_4_.1, bf16[8,32,512]{2,1,0:T(8,128)(2,1)} %refs_5_.1, bf16[8,32,512]{2,1,0:T(8,128)(2,1)} %refs_6_.1), custom_call_target="tpu_custom_call" | custom-call | tf_op jit(solution)/shard_map/pallas_call | solution.py:446
  41.2 1.5 %copy.9 = f32[1,8,4,512]{3,2,1,0:T(4,128)} copy(f32[1,8,4,512]{3,2,1,0:T(4,128)} %bitcast.1) | data formatting | bytes 131072

commit v6 on v5

--- a/solution.py
+++ b/solution.py
@@ -328,11 +328,9 @@
                 )
         near_copy(0, g).start()
 
-        @pl.when(g > 0)
-        def _():
-            pass_on(0, g - 1)
-
-    pass_on(0, groups - 1)
+    @pl.loop(0, groups)
+    def _(g):
+        pass_on(0, g)
 
     def spread_flux(g):
         whole = total(0, g)
@@ -371,23 +369,23 @@
                 put(1, g, v, start, signal_sum, depth_sum)
         near_copy(1, g).start()
 
-    @pl.loop(0, groups + 3)
+    @pl.loop(0, groups)
+    def _(g):
+        spread_flux(g)
+
+    @pl.loop(0, groups + 2)
     def _(i):
         @pl.when(i < groups)
         def _():
-            spread_flux(i)
+            share_flux(i)
 
         @pl.when((i >= 1) & (i < groups + 1))
         def _():
-            share_flux(i - 1)
-
-        @pl.when(i >= 3)
+            reweight(i - 1)
+
+        @pl.when(i >= 2)
         def _():
-            pass_on(1, i - 3)
-
-        @pl.when((i >= 2) & (i < groups + 2))
-        def _():
-            reweight(i - 2)
+            pass_on(1, i - 2)
 
     @pl.loop(0, groups)
     def _(g):

time: 42.9 us -> 41 us (0.956)
  Pallas kernels: 41.2 us -> 39.4 us
    pallas_call x1, Pallas kernels: 41.2 us -> 39.4 us  [per_device(): pl.pallas_call(functools.partial(kernel, (count, strips, exposures, rows,...]
where the time goes in v6:
time: 41 us; the launch traced here: 40.9 us
  Pallas kernels  39.4 us (96%)
  local copies, waits for them, and re-layouts  1.47 us (4%)
    pallas_call x1, Pallas kernels, per_device(): pl.pallas_call(functools.partial(kernel, (count, strips, exposures, rows,...  39.4 us
    unnamed x1, local copies, waits for them, and re-layouts  1.47 us

profile of v6, /device:TPU:0, one launch (start us, length us, event | category | flops | bytes accessed | tf_op | source)
XLA Modules:
  0.0 40.9 jit_solution(598696772962997975)
XLA Ops:
  0.0 39.4 %shard_map.73 = f32[8,4,512]{2,1,0:T(4,128)} custom-call(f32[8,9]{1,0:T(8,128)} %refs_0_.1, f32[8,9]{1,0:T(8,128)} %refs_1_.1, s32[8,8]{1,0:T(8,128)} %refs_2_.1, s32[8,8]{1,0:T(8,128)} %refs_3_.1, s32[8]{0:T(128)} %refs_4_.1, bf16[8,32,512]{2,1,0:T(8,128)(2,1)} %refs_5_.1, bf16[8,32,512]{2,1,0:T(8,128)(2,1)} %refs_6_.1), custom_call_target="tpu_custom_call" | custom-call | tf_op jit(solution)/shard_map/pallas_call | solution.py:444
  39.4 1.5 %copy.9 = f32[1,8,4,512]{3,2,1,0:T(4,128)} copy(f32[1,8,4,512]{3,2,1,0:T(4,128)} %bitcast.1) | data formatting | bytes 131072

commit v7 on v6

--- a/solution.py
+++ b/solution.py
@@ -66,7 +66,7 @@
 
     def full_copy(e, array):
         return pltpu.make_async_remote_copy(
-            src_ref=(sci, inv)[array].at[e, pl.ds(0, SHIFT)], dst_ref=below.at[array, e],
+            src_ref=inputs[5 + array].at[e, pl.ds(0, SHIFT)], dst_ref=below.at[array, e],
             send_sem=full_s.at[array, e], recv_sem=full_r.at[array, e],
             device_id={"strip": strip - 1}, device_id_type=MESH,
         )
@@ -126,6 +126,14 @@
     @pl.when(has_below)
     def _():
         pl.semaphore_signal(barrier, inc=1, device_id={"strip": strip + 1}, device_id_type=MESH)
+
+    pl.semaphore_wait(barrier, chips + has_above.astype(jnp.int32) + has_below.astype(jnp.int32))
+
+    @pl.when(has_above)
+    def _():
+        for e in (0, 1):
+            for array in (0, 1):
+                full_copy(e, array).start()
 
     for copy in local[:2]:
         copy.wait()
@@ -141,7 +149,6 @@
                     for e in span
                 ]
                 edge_out[down, array, t] = jnp.concatenate(pieces, axis=0).astype(jnp.bfloat16)
-    pl.semaphore_wait(barrier, chips + has_above.astype(jnp.int32) + has_below.astype(jnp.int32))
 
     @pl.when(has_below)
     def _():
@@ -158,8 +165,12 @@
 
             @pl.loop(0, per_tile)
             def _(q):
-                for array in (0, 1):
-                    full_copy(t * per_tile + q, array).start()
+                e = t * per_tile + q
+
+                @pl.when(e > 1)
+                def _():
+                    for array in (0, 1):
+                        full_copy(e, array).start()
 
     @pl.when(jnp.logical_not(has_above))
     def _():
@@ -475,9 +486,14 @@
             *dma(groups),
         ],
         compiler_params=pltpu.CompilerParams(
-            collective_id=0, has_side_effects=True, vmem_limit_bytes=60 * 1024 * 1024
+            collective_id=0, has_side_effects=True, vmem_limit_bytes=24 * 1024 * 1024
         ),
-    )(psf_rows, psf_cols, row_shift, col_shift, ok, science, inv_var)
+    )(
+        *(
+            pltpu.with_memory_space_constraint(x, pltpu.HBM)
+            for x in (psf_rows, psf_cols, row_shift, col_shift, ok, science, inv_var)
+        )
+    )
     return result.reshape(1, vels, own, columns)
 
 

time: 41 us -> 40 us (0.976)
  local copies, waits for them, and re-layouts: 1.47 us -> 0.63 us
    unnamed x1, local copies, waits for them, and re-layouts: 1.47 us -> 0.63 us
where the time goes in v7:
time: 40 us; the launch traced here: 39.8 us
  Pallas kernels  39.2 us (98%)
  local copies, waits for them, and re-layouts  0.63 us (2%)
    pallas_call x1, Pallas kernels, per_device(): pl.pallas_call(functools.partial(kernel, (count, strips, exposures, rows,...  39.2 us

profile of v7, /device:TPU:0, one launch (start us, length us, event | category | flops | bytes accessed | tf_op | source)
XLA Modules:
  0.0 39.8 jit_solution(6813107224532860187)
XLA Ops:
  0.0 39.2 %shard_map.73 = f32[8,4,512]{2,1,0:T(4,128)S(1)} custom-call(f32[8,9]{1,0:T(8,128)} %refs_0_.1, f32[8,9]{1,0:T(8,128)} %refs_1_.1, s32[8,8]{1,0:T(8,128)} %refs_2_.1, s32[8,8]{1,0:T(8,128)} %refs_3_.1, s32[8]{0:T(128)} %refs_4_.1, bf16[8,32,512]{2,1,0:T(8,128)(2,1)} %refs_5_.1, bf16[8,32,512]{2,1,0:T(8,128)(2,1)} %refs_6_.1), custom_call_target="tpu_custom_call" | custom-call | tf_op jit(solution)/shard_map/pallas_call | solution.py:455
  39.2 0.6 %copy.9 = f32[1,8,4,512]{3,2,1,0:T(4,128)} copy(f32[1,8,4,512]{3,2,1,0:T(4,128)S(1)} %bitcast.1) | data formatting | bytes 131072

commit v8 on v7

--- a/solution.py
+++ b/solution.py
@@ -61,6 +61,8 @@
     has_above = strip > 0
     has_below = strip < strips - 1
 
+    others = sorted(range(1, chips), key=lambda j: -min(j, chips - j))
+
     def peer(j):
         return (chip + j) % chips
 
@@ -114,7 +116,7 @@
         copy.start()
     barrier = pltpu.get_barrier_semaphore()
     pl.semaphore_signal(barrier, inc=1, device_id={"expo": sibling}, device_id_type=MESH)
-    for j in range(1, chips):
+    for j in others:
         pl.semaphore_signal(
             barrier, inc=1, device_id={"expo": peer(j) * 2 + core}, device_id_type=MESH
         )
@@ -288,10 +290,13 @@
             for copy, value in enumerate((previous_blocks(table), table, next_blocks(table))):
                 maps[which, pl.ds(copy * span + e * rows, rows)] = value
 
-        for velocity in range(vels):
-            for which in (0, 1):
-                for start in range(0, half, 8):
-                    stacks[velocity, which, pl.ds(start, 8)] += window(e, velocity, which, start)
+        @pl.when(e < exposures - 1)
+        def _():
+            for velocity in range(vels):
+                for which in (0, 1):
+                    for start in range(0, half, 8):
+                        place = velocity, which, pl.ds(start, 8)
+                        stacks[place] += window(e, velocity, which, start)
 
     def put(stage, g, v, start, signal, depth):
         for base, value in (
@@ -316,7 +321,7 @@
     def pass_on(stage, g):
         near_copy(stage, g).wait_recv()
         mine[stage][g] = sums[stage][g, core, chip] + near[stage][g, chip]
-        for j in range(1, chips):
+        for j in others:
             there = peer(j)
             both = sums[stage][g, core, there] + near[stage][g, there]
             pair[stage][g, there] = to_code(both.reshape(2, own * 8, LANES), steps)
@@ -324,7 +329,7 @@
 
     def total(stage, g):
         value = mine[stage][g]
-        for j in range(1, chips):
+        for j in others:
             far_copy(stage, g, j).wait_recv()
             value = value + from_code(far[stage][g, j - 1], steps).reshape(value.shape)
         return value
@@ -333,10 +338,12 @@
     def _(g):
         for v in (0, 1):
             for start in range(0, half, 8):
-                put(
-                    0, g, v, start,
-                    stacks[2 * g + v, 0, pl.ds(start, 8)], stacks[2 * g + v, 1, pl.ds(start, 8)],
+                signal, depth = (
+                    stacks[2 * g + v, which, pl.ds(start, 8)]
+                    + window(exposures - 1, 2 * g + v, which, start)
+                    for which in (0, 1)
                 )
+                put(0, g, v, start, signal, depth)
         near_copy(0, g).start()
 
     @pl.loop(0, groups)
@@ -348,11 +355,11 @@
         flux = whole / (roll4(whole) + 1.0)
         flux = jnp.where(low, flux[0], roll4(flux[1])).reshape(own * 8, LANES)
         fluxes[g, core, chip] = to_code(flux, steps)
-        for j in range(1, chips):
+        for j in others:
             flux_copy(g, j).start()
 
     def share_flux(g):
-        for j in range(1, chips):
+        for j in others:
             flux_copy(g, j).wait_recv()
         flux_sibling(g).start()
 
@@ -413,9 +420,9 @@
     def _(g):
         for stage in (0, 1):
             near_copy(stage, g).wait_send()
-            for j in range(1, chips):
+            for j in others:
                 far_copy(stage, g, j).wait_send()
-        for j in range(1, chips):
+        for j in others:
             flux_copy(g, j).wait_send()
         flux_sibling(g).wait_send()
 

time: 40 us -> 40.1 us (level)
  no operation moved by 1% of the time
where the time goes in v8:
time: 40.1 us
  Pallas kernels  39.5 us (99%)
  local copies, waits for them, and re-layouts  0.63 us (2%)
    pallas_call x1, Pallas kernels, per_device(): pl.pallas_call(functools.partial(kernel, (count, strips, exposures, rows,...  39.5 us

profile of v8, /device:TPU:0, one launch (start us, length us, event | category | flops | bytes accessed | tf_op | source)
XLA Modules:
  0.0 40.1 jit_solution(1362344693635305446)
XLA Ops:
  0.0 39.5 %shard_map.73 = f32[8,4,512]{2,1,0:T(4,128)S(1)} custom-call(f32[8,9]{1,0:T(8,128)} %refs_0_.1, f32[8,9]{1,0:T(8,128)} %refs_1_.1, s32[8,8]{1,0:T(8,128)} %refs_2_.1, s32[8,8]{1,0:T(8,128)} %refs_3_.1, s32[8]{0:T(128)} %refs_4_.1, bf16[8,32,512]{2,1,0:T(8,128)(2,1)} %refs_5_.1, bf16[8,32,512]{2,1,0:T(8,128)(2,1)} %refs_6_.1), custom_call_target="tpu_custom_call" | custom-call | tf_op jit(solution)/shard_map/pallas_call | solution.py:462
  39.5 0.6 %copy.9 = f32[1,8,4,512]{3,2,1,0:T(4,128)} copy(f32[1,8,4,512]{3,2,1,0:T(4,128)S(1)} %bitcast.1) | data formatting | bytes 131072

commit v9 on v7

--- a/solution.py
+++ b/solution.py
@@ -61,6 +61,8 @@
     has_above = strip > 0
     has_below = strip < strips - 1
 
+    others = sorted(range(1, chips), key=lambda j: -min(j, chips - j))
+
     def peer(j):
         return (chip + j) % chips
 
@@ -114,7 +116,7 @@
         copy.start()
     barrier = pltpu.get_barrier_semaphore()
     pl.semaphore_signal(barrier, inc=1, device_id={"expo": sibling}, device_id_type=MESH)
-    for j in range(1, chips):
+    for j in others:
         pl.semaphore_signal(
             barrier, inc=1, device_id={"expo": peer(j) * 2 + core}, device_id_type=MESH
         )
@@ -316,7 +318,7 @@
     def pass_on(stage, g):
         near_copy(stage, g).wait_recv()
         mine[stage][g] = sums[stage][g, core, chip] + near[stage][g, chip]
-        for j in range(1, chips):
+        for j in others:
             there = peer(j)
             both = sums[stage][g, core, there] + near[stage][g, there]
             pair[stage][g, there] = to_code(both.reshape(2, own * 8, LANES), steps)
@@ -324,7 +326,7 @@
 
     def total(stage, g):
         value = mine[stage][g]
-        for j in range(1, chips):
+        for j in others:
             far_copy(stage, g, j).wait_recv()
             value = value + from_code(far[stage][g, j - 1], steps).reshape(value.shape)
         return value
@@ -348,11 +350,11 @@
         flux = whole / (roll4(whole) + 1.0)
         flux = jnp.where(low, flux[0], roll4(flux[1])).reshape(own * 8, LANES)
         fluxes[g, core, chip] = to_code(flux, steps)
-        for j in range(1, chips):
+        for j in others:
             flux_copy(g, j).start()
 
     def share_flux(g):
-        for j in range(1, chips):
+        for j in others:
             flux_copy(g, j).wait_recv()
         flux_sibling(g).start()
 
@@ -413,9 +415,9 @@
     def _(g):
         for stage in (0, 1):
             near_copy(stage, g).wait_send()
-            for j in range(1, chips):
+            for j in others:
                 far_copy(stage, g, j).wait_send()
-        for j in range(1, chips):
+        for j in others:
             flux_copy(g, j).wait_send()
         flux_sibling(g).wait_send()
 

time: 40 us -> 40.3 us (level)
  no operation moved by 1% of the time
where the time goes in v9:
time: 40.3 us; the launch traced here: 40.1 us
  Pallas kernels  39.5 us (98%)
  local copies, waits for them, and re-layouts  0.63 us (2%)
    pallas_call x1, Pallas kernels, per_device(): pl.pallas_call(functools.partial(kernel, (count, strips, exposures, rows,...  39.5 us

profile of v9, /device:TPU:0, one launch (start us, length us, event | category | flops | bytes accessed | tf_op | source)
XLA Modules:
  0.0 40.1 jit_solution(2055055229881522973)
XLA Ops:
  0.0 39.5 %shard_map.73 = f32[8,4,512]{2,1,0:T(4,128)S(1)} custom-call(f32[8,9]{1,0:T(8,128)} %refs_0_.1, f32[8,9]{1,0:T(8,128)} %refs_1_.1, s32[8,8]{1,0:T(8,128)} %refs_2_.1, s32[8,8]{1,0:T(8,128)} %refs_3_.1, s32[8]{0:T(128)} %refs_4_.1, bf16[8,32,512]{2,1,0:T(8,128)(2,1)} %refs_5_.1, bf16[8,32,512]{2,1,0:T(8,128)(2,1)} %refs_6_.1), custom_call_target="tpu_custom_call" | custom-call | tf_op jit(solution)/shard_map/pallas_call | solution.py:457
  39.5 0.6 %copy.9 = f32[1,8,4,512]{3,2,1,0:T(4,128)} copy(f32[1,8,4,512]{3,2,1,0:T(4,128)S(1)} %bitcast.1) | data formatting | bytes 131072
